TPU v7x, 128 devices: a whole 4x4x4 slice. The times are simulated.
128 devices in a mesh: tower: 2 (over x_lo), dp: 64 (over x_hi, z, y, core).
Axes of the slice: x: 4 (x_hi: 2, x_lo: 2; x = x_hi * 2 + x_lo), y: 4, z: 4, core: 2. Of those that a mesh axis runs over, the one named last changes fastest.
Arguments:
- token_states: bfloat16 [2, 1024, 64, 768], P('tower', 'dp'), may hold values from -8 to 8
- qkv_weight: bfloat16 [2, 1, 768, 2304], P('tower'), may hold values from -0.21875 to 0.21875
- out_weight: bfloat16 [2, 1, 768, 768], P('tower'), may hold values from -0.21875 to 0.21875
- up_weight: bfloat16 [2, 1, 768, 3072], P('tower'), may hold values from -0.21875 to 0.21875
- down_weight: bfloat16 [2, 1, 3072, 768], P('tower'), may hold values from -0.109375 to 0.109375
- queue_states: bfloat16 [65536, 768], P(('tower', 'dp')), may hold values from -16 to 16
- queue_ids: int32 [65536], P(('tower', 'dp')), may hold values from 0 to 7
- positive: int32 [1024], replicated, may hold values from 0 to 1023, as said below
- tail_ids: int32 [1024], replicated, may hold values from 0 to 7
Outputs:
- query_loss: float32 [1024], P('dp')
- query_grad: float32 [1024, 768], P(('tower', 'dp'))
- tail_grad: float32 [1024, 768], P('dp')
Inputs may be any that keep to these rules, and one draw needn't show every extreme that they name: Each of the 1024 tails is the positive of exactly one query.
All inputs are finite; a program needn't handle non-finite values.
Results may differ from a plain program's by a relative error of at most 0.02.
Values may be sent and summed in bfloat16 or wider, within the bound.
A program may use at most 128 MiB of HBM per device.

v0:
```python
import math

import jax
import jax.numpy as jnp
from jax import lax
from jax.sharding import PartitionSpec as P

HEADS = 12
HEAD_DIM = 64


EPS_NORM = 1e-05
EPS_UNIT = 1e-06
INV_TEMP = 50.0
MARGIN = 1.0


def from_partner(value, axis, distance):
    mask = 2**distance
    pairs = [(source, source ^ mask) for source in range(lax.axis_size(axis))]
    return lax.ppermute(value, axis, pairs)


def norm_rows(values):
    average = jnp.mean(values, axis=-1, keepdims=True)
    centered = values - average
    spread = jnp.mean(centered * centered, axis=-1, keepdims=True)
    return centered / jnp.sqrt(spread + EPS_NORM)


def unit_rows(values):
    return (values / jnp.sqrt(jnp.sum(values * values, axis=-1, keepdims=True) + EPS_UNIT)).astype(
        jnp.bfloat16
    )


def encoder_layer(hidden, qkv_w, out_w, up_w, down_w):
    text_count, length, model_width = hidden.shape
    flat_in = hidden.reshape(text_count * length, model_width)
    qkv_all = jnp.dot(flat_in, qkv_w, preferred_element_type=jnp.float32).astype(jnp.bfloat16)
    qkv_all = qkv_all.reshape(text_count, length, 3, HEADS, HEAD_DIM)
    scores = jnp.einsum(
        "rshd,rthd->rhst", qkv_all[:, :, 0], qkv_all[:, :, 1], preferred_element_type=jnp.float32
    ) * (1.0 / math.sqrt(HEAD_DIM))
    exp_scores = jnp.exp(scores)
    weights_bf = (exp_scores / jnp.sum(exp_scores, axis=-1, keepdims=True)).astype(jnp.bfloat16)
    context = jnp.einsum(
        "rhst,rthd->rshd", weights_bf, qkv_all[:, :, 2], preferred_element_type=jnp.float32
    ).astype(jnp.bfloat16)
    context = context.reshape(text_count * length, model_width)
    attended = jnp.dot(context, out_w, preferred_element_type=jnp.float32)
    normed = norm_rows(flat_in.astype(jnp.float32) + attended).astype(jnp.bfloat16)
    hidden_act = jax.nn.gelu(
        jnp.dot(normed, up_w, preferred_element_type=jnp.float32), approximate=False
    ).astype(jnp.bfloat16)
    result = norm_rows(
        normed.astype(jnp.float32) + jnp.dot(hidden_act, down_w, preferred_element_type=jnp.float32)
    )
    return result.astype(jnp.bfloat16).reshape(text_count, length, model_width)


def encode(states, qkv_w, out_w, up_w, down_w):
    hidden = states
    hidden = encoder_layer(hidden, qkv_w[0], out_w[0], up_w[0], down_w[0])
    pooled = jnp.mean(hidden.astype(jnp.float32), axis=1)
    return unit_rows(pooled)


def local(
    token_states,
    qkv_weight,
    out_weight,
    up_weight,
    down_weight,
    queue_states,
    queue_ids,
    positive,
    tail_ids,
):
    own_emb = encode(token_states[0], qkv_weight[0], out_weight[0], up_weight[0], down_weight[0])
    partner = from_partner(own_emb, "tower", 0)
    is_query = lax.axis_index("tower") == 0
    query_own = jnp.where(is_query, own_emb, partner)
    tail_own = jnp.where(is_query, partner, own_emb)
    queries = lax.all_gather(query_own, "dp", axis=0, tiled=True)
    queue_keys = unit_rows(queue_states.astype(jnp.float32))
    local_rows = own_emb.shape[0]
    batch_rows = queries.shape[0]
    row_offset = lax.axis_index("dp") * local_rows
    tail_index = jnp.arange(batch_rows, dtype=jnp.int32)
    true_ids = jnp.sum(
        jnp.where(positive[:, None] == tail_index[None, :], tail_ids[None, :], 0), axis=1
    )
    local_ids = lax.dynamic_slice_in_dim(tail_ids, row_offset, local_rows)
    local_index = row_offset + jnp.arange(local_rows, dtype=jnp.int32)
    pos_mask = positive[:, None] == local_index[None, :]
    query_side = is_query.astype(jnp.float32)
    tail_scores = INV_TEMP * jnp.einsum(
        "bd,rd->br", queries, tail_own, preferred_element_type=jnp.float32
    ) - MARGIN * pos_mask.astype(jnp.float32)
    kept_mask = pos_mask | (local_ids[None, :] != true_ids[:, None])
    tail_exp = jnp.where(kept_mask, jnp.exp(tail_scores), 0.0)
    queue_scores = INV_TEMP * jnp.einsum(
        "bd,rd->br", queries, queue_keys, preferred_element_type=jnp.float32
    )
    queue_exp = jnp.where(queue_ids[None, :] != true_ids[:, None], jnp.exp(queue_scores), 0.0)
    total_part = query_side * jnp.sum(tail_exp, axis=1) + jnp.sum(queue_exp, axis=1)
    logit_part = query_side * jnp.sum(jnp.where(pos_mask, tail_scores, 0.0), axis=1)
    row_total, pos_logit = lax.psum((total_part, logit_part), ("tower", "dp"))
    query_loss = lax.dynamic_slice_in_dim(jnp.log(row_total) - pos_logit, row_offset, local_rows)
    tail_weights = (tail_exp / row_total[:, None] - pos_mask.astype(jnp.float32)).astype(
        jnp.bfloat16
    )
    queue_weights = (queue_exp / row_total[:, None]).astype(jnp.bfloat16)
    tail_grad = INV_TEMP * jnp.einsum(
        "br,bd->rd", tail_weights, queries, preferred_element_type=jnp.float32
    )
    from_tails = jnp.dot(tail_weights, tail_own, preferred_element_type=jnp.float32)
    from_queue = jnp.dot(queue_weights, queue_keys, preferred_element_type=jnp.float32)
    query_grad = lax.psum_scatter(
        INV_TEMP * (query_side * from_tails + from_queue),
        ("tower", "dp"),
        scatter_dimension=0,
        tiled=True,
    )
    return (query_loss, query_grad, tail_grad)


def solution(mesh):
    placed = (
        P("tower", "dp", None, None),
        P("tower", None, None, None),
        P("tower", None, None, None),
        P("tower", None, None, None),
        P("tower", None, None, None),
        P(("tower", "dp"), None),
        P(("tower", "dp")),
        P(),
        P(),
    )
    return jax.shard_map(
        local,
        mesh=mesh,
        in_specs=placed,
        out_specs=(P("dp"), P(("tower", "dp"), None), P("dp", None)),
        check_vma=False,
    )
```

profile of v0, /device:TPU:4, one launch (start us, length us, event | category | flops | bytes accessed | tf_op | source)
XLA Modules:
  0.0 920.8 jit_solution(17246718907739255985)
XLA Ops:
  7.2 0.0 copy-start
  7.2 0.0 all-gather.2.cloned.1.call-start
  7.2 1.9 copy-done
  9.2 7.3 convolution_convert_fusion
  16.5 6.6 copy.22
  23.1 13.2 %reshape.62 = bf16[16,64,3,12,64]{1,0,4,3,2:T(8,128)(2,1)} reshape(bf16[1024,2304]{0,1:T(8,128)(2,1)} %copy.22) | data formatting | bytes 9437184 | tf_op jit(solution)/shard_map/reshape | solution.py:41
  36.3 6.5 fusion.79
  42.8 5.1 copy.30
  47.9 3.6 copy.31
  51.5 0.0 copy-start.2
  51.5 4.8 fusion.12
  56.3 0.0 copy-done.2
  56.3 2.4 convert_bitcast_fusion
  58.8 2.4 copy.27
  61.2 3.2 reshape.63
  64.4 3.8 fusion.80
  68.3 0.5 multiply_reduce_fusion.1
  68.8 0.0 copy-start.13
  68.8 35.0 %fusion.29.clone.4 = bf16[1024,3072]{1,0:T(8,128)(2,1)S(1)} fusion(bf16[1,1,768,3072]{3,2,1,0:T(8,128)(2,1)} %param.12, f32[1024,768]{1,0:T(8,128)S(1)} %get-tuple-element.13, f32[1024]{0:T(1024)S(1)} %add_sqrt_fusion.1, f32[1024]{0:T(1024)S(1)} %broadcast_multiply_fusion.1), kind=kOutput, calls=%fused_computation.3.clone.clone.clone.clone.clone.clone.1 | convolution fusion | flops 5038669824 | bytes 14163968 | tf_op jit(solution)/shard_map/dot_general | solution.py:54
  103.8 0.0 copy-done.13
  103.8 5.3 fusion.81
  109.1 0.0 copy-start.12
  109.2 0.0 copy-start.9
  109.2 0.0 copy-start.14
  109.2 0.5 multiply_reduce_fusion
  109.7 0.6 convert_reduce_fusion
  110.3 0.1 multiply_reduce_fusion.2
  110.4 0.1 divide_convert_fusion.10
  110.5 0.0 copy-start.5
  110.5 1.3 collective-permute-start
  111.7 2.6 collective-permute-done
  114.4 0.0 copy-start.7
  114.4 0.7 broadcast_select_fusion.1
  115.1 0.0 all-gather.2.cloned.1.call-update
  115.1 0.0 reduce-scatter.2.cloned.1.call-start
  115.2 0.0 copy-done.12
  115.2 0.1 dynamic_slice.6
  115.3 0.0 copy-start.10
  115.3 1.4 fusion.30
  116.6 0.0 copy-done.9
  116.6 0.8 select_reduce_fusion
  117.4 64.7 %all-gather.2.cloned.1.call-done = bf16[1024,768]{1,0:T(8,128)(2,1)} async-done(((bf16[16,768]{1,0:T(8,128)(2,1)}), bf16[1024,768]{1,0:T(8,128)(2,1)}) %all-gather.2.cloned.1.call-update) | async-done | bytes 1572880 | tf_op jit(solution)/shard_map/all_gather | solution.py:85
  182.1 2.6 fusion.43
  184.6 0.0 copy-done.14
  184.6 2.8 fusion.84
  187.4 0.0 copy-done.5
  187.4 0.0 copy-done.7
  187.5 0.0 copy-done.10
  187.5 64.5 %all-reduce = (f32[1024]{0:T(1024)}, f32[1024]{0:T(1024)S(1)}) all-reduce(f32[1024]{0:T(1024)S(1)} %get-tuple-element.20, f32[1024]{0:T(1024)S(1)} %get-tuple-element.19), channel_id=1, replica_groups=mesh['tower'=2,'dp'=64] {'tower','dp'}, use_global_device_ids=true, to_apply=%region_13.14 | all-reduce | flops 2048 | bytes 16384 | tf_op jit(solution)/shard_map/psum | solution.py:109
  252.0 0.0 copy-done.3
  252.0 0.0 copy-start.11
  252.0 1.1 fusion.38
  253.1 0.0 copy-start.1
  253.1 0.0 copy-done.4
  253.1 0.0 copy-done.6
  253.1 0.0 copy-done.8
  253.1 0.0 copy-done.11
  253.1 2.4 add_multiply_fusion
  255.5 0.0 reduce-scatter.2.cloned.1.call-update
  255.5 0.7 log_subtract_fusion
  256.2 0.6 dynamic_slice.7
  256.8 2.4 convolution_multiply_fusion.1
  259.2 654.7 %reduce-scatter.2.cloned.1.call-done = f32[8,768]{1,0:T(8,128)} async-done(((f32[1024,768]{1,0:T(8,128)}), f32[8,768]{1,0:T(8,128)}) %reduce-scatter.2.cloned.1.call-update) | async-done | bytes 24592 | tf_op jit(solution)/shard_map/reduce_scatter | solution.py:120
  913.9 0.0 copy-done.1
  (12 shorter events, 0.1 us)
Async XLA Ops:
  7.2 2.0 copy-start
  7.2 174.9 %all-gather.2.cloned.1.call-start = ((), (), s32[]{:S(2)}) async-start(), calls=%async_computation.1 | async-start | bytes 1597440 | tf_op jit(solution)/shard_map/all_gather | solution.py:85
  51.5 4.8 copy-start.2
  68.8 35.0 %copy-start.13 = (bf16[1,1,3072,768]{3,2,1,0:T(8,128)(2,1)S(1)}, bf16[1,1,3072,768]{3,2,1,0:T(8,128)(2,1)}, u32[]{:S(2)}) copy-start(bf16[1,1,3072,768]{3,2,1,0:T(8,128)(2,1)} %param.13) | copy-start | bytes 14155780
  109.1 6.0 copy-start.12
  109.2 7.5 copy-start.9
  109.2 75.4 %copy-start.14 = (s32[512]{0:T(512)S(1)}, s32[512]{0:T(512)}, u32[]{:S(2)}) copy-start(s32[512]{0:T(512)} %param.15) | copy-start | bytes 6148
  110.5 77.0 %copy-start.5 = (bf16[16,768]{1,0:T(8,128)(2,1)}, bf16[16,768]{1,0:T(8,128)(2,1)S(1)}, u32[]{:S(2)}) copy-start(bf16[16,768]{1,0:T(8,128)(2,1)S(1)} %divide_convert_fusion.10) | copy-start | bytes 73732
  110.5 3.9 collective-permute-start
  114.4 73.1 %copy-start.7 = (bf16[16,768]{1,0:T(8,128)(2,1)}, bf16[16,768]{1,0:T(8,128)(2,1)S(1)}, u32[]{:S(2)}) copy-start(bf16[16,768]{1,0:T(8,128)(2,1)S(1)} %collective-permute-done) | copy-start | bytes 73732
  115.1 798.8 %reduce-scatter.2.cloned.1.call-start = ((), (), s32[]{:S(2)}) async-start(), calls=%async_computation.2 | async-start | bytes 3170304 | tf_op jit(solution)/shard_map/reduce_scatter | solution.py:120
  115.3 72.2 %copy-start.10 = (s32[16]{0:T(128)}, s32[16]{0:T(128)S(1)}, u32[]{:S(2)}) copy-start(s32[16]{0:T(128)S(1)} %iota_add_fusion) | copy-start | bytes 196
  184.6 67.3 %copy-start.3 = (bf16[512,768]{1,0:T(8,128)(2,1)S(1)}, bf16[512,768]{1,0:T(8,128)(2,1)}, u32[]{:S(2)}) copy-start(bf16[512,768]{1,0:T(8,128)(2,1)} %param.14) | copy-start | bytes 2359300
  252.0 1.2 copy-start.4
  252.0 1.2 copy-start.6
  252.0 1.2 copy-start.8
  252.0 1.2 copy-start.11
  253.1 660.8 %copy-start.1 = (bf16[1,1,768,2304]{3,2,1,0:T(8,128)(2,1)S(1)}, bf16[1,1,768,2304]{3,2,1,0:T(8,128)(2,1)}, u32[]{:S(2)}) copy-start(bf16[1,1,768,2304]{3,2,1,0:T(8,128)(2,1)} %param.10) | copy-start | bytes 10616836
Sparse Core Ops, SparseCore 0:
  115.2 66.7 all-gather.1
  255.6 658.2 reduce-scatter.1
where the time goes:
time: 922 us; the launch traced here: 921 us
  waiting for transfers between devices  722 us (78%)
  matrix products  70 us (8%)
  blocking collectives  64.5 us (7%)
  local copies, waits for them, and re-layouts  43.3 us (5%)
  between operations  14.3 us (2%)
    reduce_scatter x1, waiting for transfers between devices, local(): lax.psum_scatter(INV_TEMP * (query_side * from_tails + from_queue), ('tow...  655 us
    all_gather x1, waiting for transfers between devices, local(): queries = lax.all_gather(query_own, 'dp', axis=0, tiled=True)  64.7 us
    psum x1, blocking collectives, local(): row_total, pos_logit = lax.psum((total_part, logit_part), ('tower', 'dp'))  64.5 us
    dot_general x1, matrix products, encoder_layer(): jnp.dot(normed, up_w, preferred_element_type=jnp.float32)  35 us
  transfers between devices with their start and end apart: 3, of which 3 were waited for; matrix products, arithmetic and copies ran while one was open for 1% of the time, Pallas kernels for 0%

commit v1 on v0

v1 whole, which is shorter than its diff:
```python
import functools
import jax, jax.numpy as jnp
from jax import lax
from jax.experimental import pallas as pl
from jax.experimental.pallas import tpu as pltpu
from jax.sharding import PartitionSpec as P

BF = jnp.bfloat16
F32 = jnp.float32
SEQ = 64

def dot(a, b):
    return jnp.dot(a, b, preferred_element_type=F32)

def dot_t(a, b):
    return lax.dot_general(a, b, (((1,), (1,)), ((), ())), preferred_element_type=F32)

def gelu(x, kind="as"):
    if kind == "none":
        return jnp.maximum(x, 0.0)
    if kind == "erf":
        return 0.5 * x * (1.0 + lax.erf(x * 0.7071067811865476))
    a = jnp.abs(x)
    t = pl.reciprocal(1.0 + (0.3275911 * 0.7071067811865476) * a, approx=True)
    p = 0.5 * 1.061405429
    for c in (-1.453152027, 1.421413741, -0.284496736, 0.254829592):
        p = p * t + 0.5 * c
    q = p * t * jnp.exp2((x * x) * (-0.5 * 1.4426950408889634))
    return jnp.maximum(x, 0.0) - a * q

def norm_rows(v):
    avg = jnp.mean(v, axis=-1, keepdims=True)
    c = v - avg
    s = jnp.mean(c * c, axis=-1, keepdims=True)
    return c * lax.rsqrt(s + 1e-5)

def unit_rows(v):
    return v * lax.rsqrt(jnp.sum(v * v, axis=-1, keepdims=True) + 1e-6)

def enc_chunk(x, wqkv, wout, wup, wdown, waits, kind="as", fft=768, attn=True):
    m = x.shape[0]
    nt = m // SEQ
    waits[0]()
    row = lax.broadcasted_iota(jnp.int32, (256, 256), 0) // SEQ
    col = lax.broadcasted_iota(jnp.int32, (256, 256), 1) // SEQ
    ones_bd = jnp.where(row == col, 1.0, 0.0).astype(BF)
    ctx = []
    if attn:
        lane = lax.broadcasted_iota(jnp.int32, (SEQ, 128), 1)
        low = lane < 64
        zero = jnp.zeros((SEQ, 128), BF)
        def bd(t):
            a, b = t[:, :128], t[:, 128:]
            z = jnp.zeros_like(a)
            rows = [
                jnp.concatenate([jnp.where(low, a, z), zero], 1),
                jnp.concatenate([jnp.where(low, z, a), zero], 1),
                jnp.concatenate([zero, jnp.where(low, b, z)], 1),
                jnp.concatenate([zero, jnp.where(low, z, b)], 1),
            ]
            return jnp.concatenate(rows, 0)
        for g in range(3):
            q = (dot(x, wqkv[:, g * 256:(g + 1) * 256])).astype(BF) * BF(0.125)
            k = (dot(x, wqkv[:, 768 + g * 256:768 + (g + 1) * 256])).astype(BF)
            v = (dot(x, wqkv[:, 1536 + g * 256:1536 + (g + 1) * 256])).astype(BF)
            es = []
            for t in range(nt):
                sl = slice(t * SEQ, (t + 1) * SEQ)
                es.append(jnp.exp(dot_t(q[sl], bd(k[sl]))))
            e = jnp.concatenate(es, 0)
            p = (e / dot(e.astype(BF), ones_bd)).astype(BF)
            cs = []
            for t in range(nt):
                sl = slice(t * SEQ, (t + 1) * SEQ)
                cs.append(dot(p[sl], bd(v[sl])).astype(BF))
            ctx.append(jnp.concatenate(cs, 0))
        ctx = jnp.concatenate(ctx, 1)
    else:
        qkv = dot(x, wqkv[...]).astype(BF)
        ctx = qkv[:, :768] + qkv[:, 768:1536] + qkv[:, 1536:]
    waits[1]()
    normed = norm_rows(x.astype(F32) + dot(ctx, wout[...])).astype(BF)
    waits[2]()
    acc = normed.astype(F32)
    for j in range(0, 3072, fft):
        act = gelu(dot(normed, wup[:, j:j + fft]), kind).astype(BF)
        if j == 0:
            waits[3]()
        acc = acc + dot(act, wdown[j:j + fft, :])
    hid = norm_rows(acc).astype(BF).astype(F32)
    pooled = jnp.mean(hid.reshape(nt, SEQ, 768), axis=1)
    return unit_rows(pooled)

def enc_kernel(x_ref, qkv_h, out_h, up_h, down_h, o_ref, wqkv, wout, wup, wdown, sems, *, kind, fft, attn):
    step = pl.program_id(0)
    cps = [pltpu.make_async_copy(s.at[0, 0], d, sems.at[i]) for i, (s, d) in enumerate(
        [(qkv_h, wqkv), (out_h, wout), (up_h, wup), (down_h, wdown)])]
    @pl.when(step == 0)
    def _():
        for c in cps:
            c.start()
    def waiter(c):
        def f():
            @pl.when(step == 0)
            def _():
                c.wait()
        return f
    emb = enc_chunk(x_ref[0], wqkv, wout, wup, wdown, [waiter(c) for c in cps], kind, fft, attn)
    o_ref[0] = emb

def encode(x, qkv, out, up, down, m=512, kind="as", fft=768, attn=True):
    n = 1024 // m
    x = x.reshape(n, m, 768)
    return pl.pallas_call(
        functools.partial(enc_kernel, kind=kind, fft=fft, attn=attn),
        grid=(n,),
        out_shape=jax.ShapeDtypeStruct((n, m // SEQ, 768), F32),
        in_specs=[pl.BlockSpec((1, m, 768), lambda i: (i, 0, 0))] + [pl.BlockSpec(memory_space=pl.ANY)] * 4,
        out_specs=pl.BlockSpec((1, m // SEQ, 768), lambda i: (i, 0, 0)),
        scratch_shapes=[pltpu.VMEM((768, 2304), BF), pltpu.VMEM((768, 768), BF), pltpu.VMEM((768, 3072), BF),
                        pltpu.VMEM((3072, 768), BF), pltpu.SemaphoreType.DMA((4,))],
        compiler_params=pltpu.CompilerParams(vmem_limit_bytes=60 * 2**20),
    )(x, qkv, out, up, down)


MESH = pl.DeviceIdType.MESH
INV_TEMP = 50.0


def coords():
    t, dp = lax.axis_index("tower"), lax.axis_index("dp")
    core = lax.rem(dp, 2)
    y = lax.rem(lax.div(dp, 2), 4)
    z = lax.rem(lax.div(dp, 8), 4)
    x = lax.div(dp, 32) * 2 + t
    return core, (y, z, x)


def device_of(core, at):
    y, z, x = at
    return (lax.rem(x, 2), ((lax.div(x, 2) * 4 + z) * 4 + y) * 2 + core)


def moved(at, axis, step):
    return tuple(lax.rem(v + step, 4) if i == axis else v for i, v in enumerate(at))


def transpose_col(col):
    n = col.shape[0]
    return jnp.transpose(jnp.broadcast_to(col, (n, 128)))[0:1, :]


def contrast_kernel(
    emb_ref, queue_ref, qid_ref, pos_ref, tid_ref,
    loss_ref, qgrad_ref, tgrad_ref,
    gath, queries, tails, keys, parts, part_c, sum_a, part_a, sum_b, part_b, sum_d, part_d,
    tot, tot_c, tot_in,
    ag_send, ag_recv, fw_send, fw_recv, c_send, c_recv, rs_send, rs_recv, t_send, t_recv,
):
    core, at = coords()
    mate = 1 - core
    mate_dev = device_of(mate, at)
    tower, dp = lax.axis_index("tower"), lax.axis_index("dp")
    peers = [device_of(core, moved(at, axis, step)) for axis in range(3) for step in (1, 2, 3)]

    barrier = pltpu.get_barrier_semaphore()
    for dev in peers + [mate_dev]:
        pl.semaphore_signal(barrier, inc=1, device_id=dev, device_id_type=MESH)

    sends = []

    def send(src, dst, ssem, rsem, dev):
        c = pltpu.make_async_remote_copy(src_ref=src, dst_ref=dst, send_sem=ssem, recv_sem=rsem, device_id=dev, device_id_type=MESH)
        c.start()
        sends.append(c)

    def arrive(dst, ssem, rsem):
        pltpu.make_async_remote_copy(src_ref=dst, dst_ref=dst, send_sem=ssem, recv_sem=rsem, device_id=mate_dev, device_id_type=MESH).wait_recv()

    order = [[k, (k + 1) % 3, (k + 2) % 3] for k in range(3)]
    idx = [[at[a] for a in order[k]] for k in range(3)]

    for k in range(3):
        gath[k, core, idx[k][2], idx[k][1], idx[k][0]] = emb_ref[:, k * 256:(k + 1) * 256].astype(BF)

    pl.semaphore_wait(barrier, 10)

    def piece(k, stage, who, step):
        i0, i1, i2 = idx[k]
        if stage == 0:
            return gath.at[k, who, i2, i1, lax.rem(i0 + step, 4)]
        if stage == 1:
            return gath.at[k, who, i2, lax.rem(i1 + step, 4)]
        return gath.at[k, who, lax.rem(i2 + step, 4)]

    for stage in range(3):
        for k in range(3):
            src = piece(k, stage, core, 0)
            for step in (1, 2, 3):
                send(src, src, ag_send.at[k, stage, step - 1], ag_recv.at[k, stage, step - 1],
                     device_of(core, moved(at, order[k][stage], step)))
            if stage > 0:
                if stage == 1:
                    send(src, src, fw_send.at[k, 0], fw_recv.at[k, 0], mate_dev)
                else:
                    for step in (1, 2, 3):
                        p = piece(k, 1, core, step)
                        send(p, p, fw_send.at[k, step], fw_recv.at[k, step], mate_dev)
        if stage == 0:
            def key_rows(i, _):
                rows = pl.ds(pl.multiple_of(i * 128, 128), 128)
                keys[rows, :] = unit_rows(queue_ref[rows, :].astype(F32)).astype(BF)
                return 0
            lax.fori_loop(0, 4, key_rows, 0)
        for k in range(3):
            for step in (1, 2, 3):
                arrive(piece(k, stage, core, 4 - step), ag_send.at[k, stage, step - 1], ag_recv.at[k, stage, step - 1])
                if stage == 2:
                    p = piece(k, 2, core, 4 - step)
                    send(p, p, fw_send.at[k, 3 + step], fw_recv.at[k, 3 + step], mate_dev)
    for k in range(3):
        arrive(piece(k, 1, mate, 0), fw_send.at[k, 0], fw_recv.at[k, 0])
        for step in (1, 2, 3):
            p = piece(k, 1, mate, step)
            arrive(p, fw_send.at[k, step], fw_recv.at[k, step])
            p = piece(k, 2, mate, 4 - step)
            arrive(p, fw_send.at[k, 3 + step], fw_recv.at[k, 3 + step])

    def assemble(n, _):
        y, z, xh = lax.rem(n, 4), lax.rem(lax.div(n, 4), 4), lax.div(n, 16)
        for who in range(2):
            rows = pl.ds(pl.multiple_of(n * 32 + who * 16, 16), 16)
            for side, dst in ((0, queries), (1, tails)):
                place = (y, z, 2 * xh + side)
                for k in range(3):
                    j0, j1, j2 = (place[a] for a in order[k])
                    dst[rows, k * 256:(k + 1) * 256] = gath[k, who, j2, j1, j0]
        return 0

    lax.fori_loop(0, 32, assemble, 0)

    pos = pos_ref[...]
    tid = tid_ref[...].astype(F32)
    true_row = jnp.zeros((1, 1024), F32)
    for j in range(0, 1024, 256):
        hot = (lax.broadcasted_iota(jnp.int32, (256, 1024), 0) + j == pos).astype(F32).astype(BF)
        true_row = true_row + dot(jnp.broadcast_to(tid[:, j:j + 256], (16, 256)).astype(BF), hot)[0:1, :]
    true_col = jnp.transpose(jnp.broadcast_to(true_row, (128, 1024)))[:, 0:1]
    qid = qid_ref[...].astype(F32)

    base = dp * 16
    own_tails = tails[pl.ds(pl.multiple_of(base, 16), 16), :]
    all_queries = queries[...]
    lane = lax.broadcasted_iota(jnp.int32, (16, 1024), 1)
    row = lax.broadcasted_iota(jnp.int32, (16, 1024), 0)
    own_ids = jnp.sum(jnp.where(lane == base + row, tid, 0.0), axis=1, keepdims=True)
    is_pos = pos == base + row
    tail_scores = INV_TEMP * dot_t(own_tails, all_queries) - is_pos.astype(F32)
    tail_exp = jnp.where(is_pos | (own_ids != true_row), jnp.exp(tail_scores), 0.0)
    side = jnp.where(tower == 0, 1.0, 0.0).astype(F32)
    negative = (jnp.where(is_pos, 0.0, tail_exp) * side)
    tot_row = jnp.sum(tail_exp, axis=0, keepdims=True) * side
    key_rows_bf = keys[...]
    queue_rows = []
    for xc in range(4):
        rows = slice(xc * 256, (xc + 1) * 256)
        x_at = 2 * (xc % 2) + xc // 2
        s = INV_TEMP * dot_t(all_queries[rows], key_rows_bf)
        e = jnp.where(true_col[rows] != qid, jnp.exp(s), 0.0)
        queue_rows.append(transpose_col(jnp.sum(e, axis=1, keepdims=True)))
        neg = jnp.transpose(negative[:, rows])
        u = dot(e.astype(BF), key_rows_bf) + dot(neg.astype(BF), own_tails)
        u = u.reshape(4, 4, 2, 8, 768)
        for z in range(4):
            for y in range(4):
                for who in range(2):
                    place = (y, z, x_at)
                    for k in range(3):
                        j0, j1, j2 = (place[a] for a in order[k])
                        blk = jnp.concatenate([u[z, y, who, :, k * 256:k * 256 + 128], u[z, y, who, :, k * 256 + 128:k * 256 + 256]], axis=0)
                        parts[k, who, j2, j1, j0] = blk.astype(BF)
    tot[0] = tot_row + jnp.concatenate(queue_rows, axis=1)

    for k in range(3):
        send(parts.at[k, mate], part_c.at[k], c_send.at[k], c_recv.at[k], mate_dev)
    send(tot.at[0], tot_c, t_send.at[0, 0], t_recv.at[0, 0], mate_dev)

    lane = lax.broadcasted_iota(jnp.int32, (32, 1024), 1)
    row = lax.broadcasted_iota(jnp.int32, (32, 1024), 0)
    start = tower * 512 + dp * 8
    want = jnp.where(row < 16, start + row, base + row - 16)
    sel = lane == want
    own_q = dot(sel.astype(F32).astype(BF), all_queries)
    own_pos = jnp.sum(jnp.where(sel, pos.astype(F32), 0.0), axis=1, keepdims=True).astype(jnp.int32)
    pos_emb = dot((lane == own_pos).astype(F32).astype(BF), tails[...])
    logit = INV_TEMP * jnp.sum(own_q * pos_emb, axis=1, keepdims=True) - 1.0

    arrive(tot_c, t_send.at[0, 0], t_recv.at[0, 0])
    total = tot[0] + tot_c[...]
    for axis in range(3):
        tot[axis + 1] = total
        for step in (1, 2, 3):
            send(tot.at[axis + 1], tot_in.at[axis, step - 1], t_send.at[axis + 1, step - 1], t_recv.at[axis + 1, step - 1],
                 device_of(core, moved(at, axis, step)))
        if axis == 0:
            for k in range(3):
                arrive(part_c.at[k], c_send.at[k], c_recv.at[k])
                sum_a[k] = (parts[k, core].astype(F32) + part_c[k].astype(F32)).astype(BF)
                i2 = idx[k][2]
                for step in (1, 2, 3):
                    send(sum_a.at[k, lax.rem(i2 + step, 4)], part_a.at[k, step - 1], rs_send.at[k, 0, step - 1], rs_recv.at[k, 0, step - 1],
                         device_of(core, moved(at, order[k][2], step)))
        elif axis == 1:
            for k in range(3):
                for step in (1, 2, 3):
                    arrive(part_a.at[k, step - 1], rs_send.at[k, 0, step - 1], rs_recv.at[k, 0, step - 1])
                acc = sum_a[k, idx[k][2]].astype(F32)
                for step in range(3):
                    acc = acc + part_a[k, step].astype(F32)
                sum_b[k] = acc.astype(BF)
                for step in (1, 2, 3):
                    send(sum_b.at[k, lax.rem(idx[k][1] + step, 4)], part_b.at[k, step - 1], rs_send.at[k, 1, step - 1], rs_recv.at[k, 1, step - 1],
                         device_of(core, moved(at, order[k][1], step)))
        else:
            for k in range(3):
                for step in (1, 2, 3):
                    arrive(part_b.at[k, step - 1], rs_send.at[k, 1, step - 1], rs_recv.at[k, 1, step - 1])
                acc = sum_b[k, idx[k][1]].astype(F32)
                for step in range(3):
                    acc = acc + part_b[k, step].astype(F32)
                sum_d[k] = acc.astype(BF)
                for step in (1, 2, 3):
                    send(sum_d.at[k, lax.rem(idx[k][0] + step, 4)], part_d.at[k, step - 1], rs_send.at[k, 2, step - 1], rs_recv.at[k, 2, step - 1],
                         device_of(core, moved(at, order[k][0], step)))
        for step in (1, 2, 3):
            arrive(tot_in.at[axis, step - 1], t_send.at[axis + 1, step - 1], t_recv.at[axis + 1, step - 1])
        total = total + tot_in[axis, 0] + tot_in[axis, 1] + tot_in[axis, 2]

    weights = (tail_exp / total - is_pos.astype(F32)).astype(BF)
    tgrad_ref[...] = INV_TEMP * dot(weights, all_queries)
    own_total = jnp.sum(jnp.where(sel, total, 0.0), axis=1, keepdims=True)
    loss = jnp.log(own_total[16:]) - logit[16:]
    eye = lax.broadcasted_iota(jnp.int32, (16, 16), 0) == lax.broadcasted_iota(jnp.int32, (16, 16), 1)
    loss_ref[...] = jnp.sum(jnp.where(eye, loss, 0.0), axis=0, keepdims=True)
    excess = jnp.exp(logit[:8]) / own_total[:8] - 1.0
    cols = []
    for k in range(3):
        for step in (1, 2, 3):
            arrive(part_d.at[k, step - 1], rs_send.at[k, 2, step - 1], rs_recv.at[k, 2, step - 1])
        acc = sum_d[k, idx[k][0]].astype(F32)
        for step in range(3):
            acc = acc + part_d[k, step].astype(F32)
        cols += [acc[:8], acc[8:]]
    u = jnp.concatenate(cols, axis=1)
    qgrad_ref[...] = INV_TEMP * (u / own_total[:8] + excess * pos_emb[:8])
    for c in sends:
        c.wait_send()


def contrast(emb, queue_states, queue_ids, positive, tail_ids):
    vm = pl.BlockSpec(memory_space=pltpu.VMEM)
    dma = pltpu.SemaphoreType.DMA
    loss, qgrad, tgrad = pl.pallas_call(
        contrast_kernel,
        out_shape=(
            jax.ShapeDtypeStruct((1, 16), F32),
            jax.ShapeDtypeStruct((8, 768), F32),
            jax.ShapeDtypeStruct((16, 768), F32),
        ),
        in_specs=[vm] * 5,
        out_specs=(vm, vm, vm),
        scratch_shapes=[
            pltpu.VMEM((3, 2, 4, 4, 4, 16, 256), BF),
            pltpu.VMEM((1024, 768), BF),
            pltpu.VMEM((1024, 768), BF),
            pltpu.VMEM((512, 768), BF),
            pltpu.VMEM((3, 2, 4, 4, 4, 16, 128), BF),
            pltpu.VMEM((3, 4, 4, 4, 16, 128), BF),
            pltpu.VMEM((3, 4, 4, 4, 16, 128), BF),
            pltpu.VMEM((3, 3, 4, 4, 16, 128), BF),
            pltpu.VMEM((3, 4, 4, 16, 128), BF),
            pltpu.VMEM((3, 3, 4, 16, 128), BF),
            pltpu.VMEM((3, 4, 16, 128), BF),
            pltpu.VMEM((3, 3, 16, 128), BF),
            pltpu.VMEM((4, 1, 1024), F32),
            pltpu.VMEM((1, 1024), F32),
            pltpu.VMEM((3, 3, 1, 1024), F32),
            dma((3, 3, 3)), dma((3, 3, 3)),
            dma((3, 7)), dma((3, 7)),
            dma((3,)), dma((3,)),
            dma((3, 3, 3)), dma((3, 3, 3)),
            dma((4, 3)), dma((4, 3)),
        ],
        compiler_params=pltpu.CompilerParams(
            collective_id=0, has_side_effects=True, vmem_limit_bytes=48 * 2**20
        ),
    )(emb, queue_states, queue_ids.reshape(1, 512), positive.reshape(1, 1024), tail_ids.reshape(1, 1024))
    return loss.reshape(16), qgrad, tgrad


def local(token_states, qkv_weight, out_weight, up_weight, down_weight, queue_states, queue_ids, positive, tail_ids):
    emb = encode(token_states[0], qkv_weight, out_weight, up_weight, down_weight).reshape(16, 768)
    return contrast(emb, queue_states, queue_ids, positive, tail_ids)


def solution(mesh):
    placed = (
        P("tower", "dp", None, None),
        P("tower", None, None, None),
        P("tower", None, None, None),
        P("tower", None, None, None),
        P("tower", None, None, None),
        P(("tower", "dp"), None),
        P(("tower", "dp")),
        P(),
        P(),
    )
    return jax.shard_map(
        local,
        mesh=mesh,
        in_specs=placed,
        out_specs=(P("dp"), P(("tower", "dp"), None), P("dp", None)),
        check_vma=False,
    )
```

time: 922 us -> 77.8 us (0.08)
  the two profiles are of different devices: /device:TPU:4 before, /device:TPU:0 now
where the time goes in v1:
time: 77.8 us; the launch traced here: 77.6 us
  Pallas kernels  74.3 us (96%)
  local copies, waits for them, and re-layouts  2.55 us (3%)
    pallas_call x1, Pallas kernels, contrast(): pl.pallas_call(contrast_kernel, out_shape=(jax.ShapeDtypeStruct((1, 16),...  42.6 us
    pallas_call x1, Pallas kernels, encode(): pl.pallas_call(functools.partial(enc_kernel, kind=kind, fft=fft, attn=att...  31.7 us
    unnamed x13, local copies, waits for them, and re-layouts  2.55 us

profile of v1, /device:TPU:0, one launch (start us, length us, event | category | flops | bytes accessed | tf_op | source)
XLA Modules:
  0.0 77.6 jit_solution(3958882446090814513)
XLA Ops:
  0.6 0.0 copy-start
  0.6 0.0 copy-start.2
  0.7 0.0 copy-start.3
  0.7 0.0 copy-start.4
  0.7 31.7 %shard_map.112 = f32[2,8,768]{2,1,0:T(8,128)} custom-call(bf16[2,512,768]{2,1,0:T(8,128)(2,1)} %bitcast.11, bf16[1,1,768,2304]{3,2,1,0:T(8,128)(2,1)} %qkv_h.1, bf16[1,1,768,768]{3,2,1,0:T(8,128)(2,1)} %out_h.1, bf16[1,1,768,3072]{3,2,1,0:T(8,128)(2,1)} %up_h.1, bf16[1,1,3072,768]{3,2,1,0:T(8,128)(2,1)} %down_h.1), custom_call_target="tpu_custom_call" | custom-call | tf_op jit(solution)/shard_map/pallas_call | solution.py:114
  32.4 0.0 copy-done
  32.4 0.0 copy-done.2
  32.4 0.0 copy-done.3
  32.4 0.0 copy-done.4
  32.4 0.0 copy-start.1
  32.4 0.8 %copy-done.1 = f32[2,8,768]{2,1,0:T(8,128)S(1)} copy-done((f32[2,8,768]{2,1,0:T(8,128)S(1)}, f32[2,8,768]{2,1,0:T(8,128)}, u32[]{:S(2)}) %copy-start.1) | copy-done | bytes 49176
  33.2 42.6 %shard_map.113 = (f32[1,16]{1,0:T(1,128)S(1)}, f32[8,768]{1,0:T(8,128)S(1)}, f32[16,768]{1,0:T(8,128)S(1)}) custom-call(f32[16,768]{1,0:T(8,128)S(1)} %bitcast.6, bf16[512,768]{1,0:T(8,128)(2,1)S(1)} %copy-done, s32[1,512]{1,0:T(1,128)S(1)} %bitcast.9, s32[1,1024]{1,0:T(1,128)S(1)} %bitcast.7, s32[1,1024]{1,0:T(1,128)S(1)} %bitcast.8), custom_call_target="tpu_custom_call" | custom-call | tf_op jit(solution)/shard_map/pallas_call | solution.py:363
  75.9 0.5 copy.15
  76.4 0.6 copy.16
  77.0 0.6 copy.17
Async XLA Ops:
  0.6 31.8 %copy-start = (bf16[512,768]{1,0:T(8,128)(2,1)S(1)}, bf16[512,768]{1,0:T(8,128)(2,1)}, u32[]{:S(2)}) copy-start(bf16[512,768]{1,0:T(8,128)(2,1)} %queue_ref.1) | copy-start | bytes 2359300
  0.6 31.8 %copy-start.2 = (s32[1024]{0:T(1024)S(1)}, s32[1024]{0:T(1024)}, u32[]{:S(2)}) copy-start(s32[1024]{0:T(1024)} %param.16) | copy-start | bytes 12292
  0.7 31.8 %copy-start.3 = (s32[1024]{0:T(1024)S(1)}, s32[1024]{0:T(1024)}, u32[]{:S(2)}) copy-start(s32[1024]{0:T(1024)} %param.17) | copy-start | bytes 12292
  0.7 31.8 %copy-start.4 = (s32[512]{0:T(512)S(1)}, s32[512]{0:T(512)}, u32[]{:S(2)}) copy-start(s32[512]{0:T(512)} %param.15) | copy-start | bytes 6148
  32.4 0.8 %copy-start.1 = (f32[2,8,768]{2,1,0:T(8,128)S(1)}, f32[2,8,768]{2,1,0:T(8,128)}, u32[]{:S(2)}) copy-start(f32[2,8,768]{2,1,0:T(8,128)} %shard_map.112) | copy-start | bytes 147460

commit v2 on v0

v2 whole, which is shorter than its diff:
```python
import functools
import jax, jax.numpy as jnp
from jax import lax
from jax.experimental import pallas as pl
from jax.experimental.pallas import tpu as pltpu
from jax.sharding import PartitionSpec as P

BF = jnp.bfloat16
F32 = jnp.float32
SEQ = 64

def dot(a, b):
    return jnp.dot(a, b, preferred_element_type=F32)

def dot_t(a, b):
    return lax.dot_general(a, b, (((1,), (1,)), ((), ())), preferred_element_type=F32)

def gelu(x):
    a = jnp.abs(x)
    t = pl.reciprocal(1.0 + (0.3275911 * 0.7071067811865476) * a, approx=True)
    p = 0.5 * 1.061405429
    for c in (-1.453152027, 1.421413741, -0.284496736, 0.254829592):
        p = p * t + 0.5 * c
    q = p * t * jnp.exp2((x * x) * (-0.5 * 1.4426950408889634))
    return jnp.maximum(x, 0.0) - a * q

def norm_rows(v):
    avg = jnp.mean(v, axis=-1, keepdims=True)
    c = v - avg
    s = jnp.mean(c * c, axis=-1, keepdims=True)
    return c * lax.rsqrt(s + 1e-5)

def unit_rows(v):
    return v * lax.rsqrt(jnp.sum(v * v, axis=-1, keepdims=True) + 1e-6)

def enc_chunk(x, wqkv, wout, wup, wdown, waits, mid, fft=768):
    m = x.shape[0]
    nt = m // SEQ
    waits[0]()
    row = lax.broadcasted_iota(jnp.int32, (256, 256), 0) // SEQ
    col = lax.broadcasted_iota(jnp.int32, (256, 256), 1) // SEQ
    ones_bd = jnp.where(row == col, 1.0, 0.0).astype(BF)
    ctx = []
    lane = lax.broadcasted_iota(jnp.int32, (SEQ, 128), 1)
    low = lane < 64
    zero = jnp.zeros((SEQ, 128), BF)
    def bd(t):
        a, b = t[:, :128], t[:, 128:]
        z = jnp.zeros_like(a)
        rows = [
            jnp.concatenate([jnp.where(low, a, z), zero], 1),
            jnp.concatenate([jnp.where(low, z, a), zero], 1),
            jnp.concatenate([zero, jnp.where(low, b, z)], 1),
            jnp.concatenate([zero, jnp.where(low, z, b)], 1),
        ]
        return jnp.concatenate(rows, 0)
    for g in range(3):
        q = (dot(x, wqkv[:, g * 256:(g + 1) * 256])).astype(BF) * BF(0.125)
        k = (dot(x, wqkv[:, 768 + g * 256:768 + (g + 1) * 256])).astype(BF)
        v = (dot(x, wqkv[:, 1536 + g * 256:1536 + (g + 1) * 256])).astype(BF)
        es = []
        for t in range(nt):
            sl = slice(t * SEQ, (t + 1) * SEQ)
            es.append(jnp.exp(dot_t(q[sl], bd(k[sl]))))
        e = jnp.concatenate(es, 0)
        p = (e / dot(e.astype(BF), ones_bd)).astype(BF)
        cs = []
        for t in range(nt):
            sl = slice(t * SEQ, (t + 1) * SEQ)
            cs.append(dot(p[sl], bd(v[sl])).astype(BF))
        ctx.append(jnp.concatenate(cs, 0))
    ctx = jnp.concatenate(ctx, 1)
    waits[1]()
    normed = norm_rows(x.astype(F32) + dot(ctx, wout[...])).astype(BF)
    waits[2]()
    acc = normed.astype(F32)
    for j in range(0, 3072, fft):
        act = gelu(dot(normed, wup[:, j:j + fft])).astype(BF)
        if j == 0:
            waits[3]()
        acc = acc + dot(act, wdown[j:j + fft, :])
        mid(j // fft)
    hid = norm_rows(acc).astype(BF).astype(F32)
    pooled = jnp.mean(hid.reshape(nt, SEQ, 768), axis=1)
    return unit_rows(pooled)

MESH = pl.DeviceIdType.MESH
INV_TEMP = 50.0


def pack(rows):
    return jnp.concatenate([rows[:, j * 128:(j + 1) * 128] for j in range(6)], axis=0)


def unpack(blocks):
    n = blocks.shape[0]
    parts = blocks.reshape(n, 6, 8, 128)
    return jnp.concatenate([parts[:, j].reshape(n * 8, 128) for j in range(6)], axis=1)


def to_row(col):
    n = col.shape[0]
    return jnp.transpose(jnp.broadcast_to(col, (n, 128)))[0:1, :]


def iota(shape, dim):
    return lax.broadcasted_iota(jnp.int32, shape, dim)


def hot(mask):
    return mask.astype(F32).astype(BF)


def step_kernel(
    x_hbm, qkv_h, out_h, up_h, down_h, queue_ref, qid_ref, pos_ref, tid_ref,
    loss_ref, qgrad_ref, tgrad_ref,
    wqkv, wout, wup, wdown, xs, keys, qids, ids, true_col, own_pack, mate_pack,
    gq, gt, queries, tails, ubuf, rbuf, qtot, tail_exp, tot_out, tot_in, grad_out, grad_in, tg_out, tg_in,
    w_sem, x_sem, agq_recv, agt_recv, ag_send, rs_send, rs_recv, tot_send, tot_recv, m_send, m_recv,
):
    tower, dp = lax.axis_index("tower"), lax.axis_index("dp")
    core, chip = lax.rem(dp, 2), lax.div(dp, 2)
    place = tower * 32 + chip
    mate = 1 - core
    mate_dev = (tower, chip * 2 + mate)
    handler = lax.rem(chip, 2) == core

    def same_core(n):
        return (lax.div(n, 32), lax.rem(n, 32) * 2 + core)

    def loop(first, last, body):
        def f(i, _):
            body(i)
            return 0
        lax.fori_loop(first, last, f, 0)

    barrier = pltpu.get_barrier_semaphore()
    loop(1, 64, lambda j: pl.semaphore_signal(barrier, inc=1, device_id=same_core(lax.rem(place + j, 64)), device_id_type=MESH))
    pl.semaphore_signal(barrier, inc=1, device_id=mate_dev, device_id_type=MESH)

    loads = [pltpu.make_async_copy(s.at[0, 0], d, w_sem.at[i]) for i, (s, d) in enumerate(
        [(qkv_h, wqkv), (out_h, wout), (up_h, wup), (down_h, wdown)])]
    x_loads = [pltpu.make_async_copy(x_hbm.at[h], xs.at[h], x_sem.at[h]) for h in range(2)]
    x_loads[0].start()
    for c in loads:
        c.start()
    x_loads[1].start()

    def remote(src, dst, ssem, rsem, dev):
        return pltpu.make_async_remote_copy(src_ref=src, dst_ref=dst, send_sem=ssem, recv_sem=rsem, device_id=dev, device_id_type=MESH)

    def key_rows(i):
        rows = pl.ds(pl.multiple_of(i * 128, 128), 128)
        keys[0, rows, :] = unit_rows(queue_ref[rows, :].astype(F32)).astype(BF)
    loop(0, 4, key_rows)
    qids[0] = qid_ref[...]
    pos = pos_ref[...]
    tid = tid_ref[...].astype(F32)
    true_row = jnp.zeros((1, 1024), F32)
    for j in range(0, 1024, 256):
        true_row = true_row + dot(jnp.broadcast_to(tid[:, j:j + 256], (16, 256)).astype(BF), hot(iota((256, 1024), 0) + j == pos))[0:1, :]
    pos_hi = lax.div(pos, 32)
    mixed = jnp.concatenate([jnp.broadcast_to(v, (8, 1024)) for v in (pos_hi.astype(F32), (pos - 32 * pos_hi).astype(F32), true_row, true_row)], axis=0).astype(BF)
    for h in range(2):
        p = iota((1024, 256), 1)
        source = (lax.div(p, 8) * 2 + core) * 16 + h * 8 + lax.rem(p, 8)
        got = dot(mixed, hot(iota((1024, 256), 0) == source))
        ids[0:1, h * 256:(h + 1) * 256] = got[0:1] * 32.0 + got[8:9]
        ids[1:2, h * 256:(h + 1) * 256] = got[16:17]
        true_col[h * 256:(h + 1) * 256, :] = jnp.transpose(jnp.broadcast_to(got[16:17], (128, 256)))

    def gather_wait(h, side, buf, sems):
        def one(s):
            @pl.when(jnp.logical_not((tower == side) & (s == chip)))
            def _():
                remote(buf.at[s], buf.at[s], ag_send.at[h, 0], sems.at[h, s], mate_dev).wait_recv()
        loop(0, 32, one)

    def gather_start(h):
        def to_all(dst, sems):
            def one(j):
                remote(own_pack.at[h], dst, ag_send.at[h, j], sems.at[h, chip], same_core(lax.rem(place + j, 64))).start()
            loop(1, 64, one)
        @pl.when(tower == 0)
        def _():
            gq[h, chip] = own_pack[h]
            to_all(gq.at[h, chip], agq_recv)
        @pl.when(tower == 1)
        def _():
            gt[h, core, chip] = own_pack[h]
            to_all(gt.at[h, core, chip], agt_recv)
        remote(own_pack.at[h], mate_pack.at[h], m_send.at[h], m_recv.at[h], mate_dev).start()

    def queue_part(h):
        gather_wait(h, 0, gq.at[h], agq_recv)
        q = unpack(gq[h].astype(F32)).astype(BF)
        queries[pl.ds(h * 256, 256), :] = q
        total = jnp.zeros((256, 1), F32)
        u = jnp.zeros((256, 768), F32)
        truth = true_col[pl.ds(h * 256, 256), 0:1]
        for who in range(2):
            k = keys[who]
            s = INV_TEMP * dot_t(q, k)
            e = jnp.where(truth != qids[who].astype(F32), jnp.exp(s), 0.0)
            total = total + jnp.sum(e, axis=1, keepdims=True)
            u = u + dot(e.astype(BF), k)
        qtot[h] = to_row(total)
        for s in range(32):
            ubuf[h, s] = pack(u[s * 8:(s + 1) * 8]).astype(BF)
        def one(s):
            dest = lax.div(s, 16) * 32 + lax.rem(2 * s + core, 32)
            @pl.when(dest == place)
            def _():
                rbuf[h, place] = ubuf[h, s]
            @pl.when(dest != place)
            def _():
                remote(ubuf.at[h, s], rbuf.at[h, place], rs_send.at[h, s], rs_recv.at[h, place], same_core(dest)).start()
        loop(0, 32, one)

    keys_copy = remote(keys.at[0], keys.at[1], m_send.at[2], m_recv.at[2], mate_dev)
    qids_copy = remote(qids.at[0], qids.at[1], m_send.at[3], m_recv.at[3], mate_dev)

    def half(h):
        def waiter(c):
            def f():
                @pl.when(h == 0)
                def _():
                    c.wait()
                    if c is loads[1]:
                        pl.semaphore_wait(barrier, 64)
            return f
        def mid(j):
            if j == MID:
                @pl.when(h == 1)
                def _():
                    keys_copy.wait_recv()
                    qids_copy.wait_recv()
                    queue_part(0)
        pltpu.make_async_copy(x_hbm.at[h], xs.at[h], x_sem.at[h]).wait()
        emb = enc_chunk(xs[h], wqkv, wout, wup, wdown, [waiter(c) for c in loads], mid)
        own_pack[h] = pack(emb).astype(BF)
        @pl.when(h == 0)
        def _():
            keys_copy.start()
            qids_copy.start()
        gather_start(h)
    loop(0, 2, half)

    def pack_wait(h):
        remote(mate_pack.at[h], mate_pack.at[h], m_send.at[h], m_recv.at[h], mate_dev).wait_recv()
    pack_wait(0)
    pack_wait(1)
    queue_part(1)

    pos_q, true_q = ids[0:1, :].astype(jnp.int32), ids[1:2, :]
    row = iota((32, 512), 0)
    is_pos = pos_q == chip * 32 + row
    chip_ids = jnp.sum(jnp.where(iota((32, 1024), 1) == chip * 32 + iota((32, 1024), 0), tid, 0.0), axis=1, keepdims=True)

    def tail_scores(mine, other):
        mine, other = unpack(mine), unpack(other)
        first = jnp.where(core == 0, mine, other)
        second = jnp.where(core == 0, other, mine)
        t32 = jnp.concatenate([first, second], axis=0).astype(BF)
        s = INV_TEMP * dot_t(t32, queries[...]) - is_pos.astype(F32)
        tail_exp[...] = jnp.where(is_pos | (chip_ids != true_q), jnp.exp(s), 0.0)

    total = jnp.concatenate([qtot[0], qtot[1]], axis=1)
    @pl.when(tower == 1)
    def _():
        tail_scores(own_pack[...].astype(F32), mate_pack[...].astype(F32))
    tail_part = jnp.sum(tail_exp[...], axis=0, keepdims=True)
    tot_out[...] = total + jnp.where(tower == 1, tail_part, 0.0)
    tot_in[place] = tot_out[...]
    loop(1, 64, lambda j: remote(tot_out, tot_in.at[place], tot_send.at[j], tot_recv.at[place], same_core(lax.rem(place + j, 64))).start())

    for h in range(2):
        gather_wait(h, 1, gt.at[h, core], agt_recv)
        remote(gt.at[h, core], gt.at[h, core], m_send.at[4 + h], m_recv.at[4 + h], mate_dev).start()
    for h in range(2):
        remote(gt.at[h, mate], gt.at[h, mate], m_send.at[4 + h], m_recv.at[4 + h], mate_dev).wait_recv()
    @pl.when(tower == 0)
    def _():
        tail_scores(gt[:, core, chip].astype(F32), gt[:, mate, chip].astype(F32))
    for who in range(2):
        halves = [unpack(gt[h, who].astype(F32)).reshape(32, 8, 768) for h in range(2)]
        tails[:, who] = jnp.concatenate(halves, axis=1).astype(BF)
    all_tails = tails[...].reshape(1024, 768)

    rows = iota((32, 1024), 0)
    lane = iota((32, 1024), 1)
    own = jnp.where(rows < 16, place * 16 + rows, dp * 16 + rows - 16)
    sel = lane == own
    own_pos = jnp.sum(jnp.where(sel, pos.astype(F32), 0.0), axis=1, keepdims=True).astype(jnp.int32)
    own_true = jnp.sum(jnp.where(sel, true_row, 0.0), axis=1, keepdims=True)
    def query_rows(d):
        return jnp.concatenate([unpack(gq[h, pl.ds(lax.div(d, 2), 1)].astype(F32)) for h in range(2)], axis=0)
    own_q = jnp.concatenate([query_rows(place), query_rows(dp)], axis=0)
    at_pos = lane == own_pos
    pos_emb = dot(hot(at_pos), all_tails)
    logit = INV_TEMP * jnp.sum(own_q * pos_emb, axis=1, keepdims=True) - 1.0
    own_s = INV_TEMP * dot_t(own_q[:16].astype(BF), all_tails)
    own_e = jnp.where(at_pos[:16] | (tid == own_true[:16]), 0.0, jnp.exp(own_s))
    from_tails = dot(own_e.astype(BF), all_tails)

    def tot_wait(s):
        @pl.when(s != place)
        def _():
            remote(tot_in.at[s], tot_in.at[s], tot_send.at[0], tot_recv.at[s], mate_dev).wait_recv()
    loop(0, 64, tot_wait)
    total = jnp.sum(tot_in[...], axis=0)

    weights = (tail_exp[...] / total - is_pos.astype(F32)).astype(BF)
    tg_out[...] = (INV_TEMP * dot(weights, queries[...])).reshape(2, 16, 768)
    tg_copy = remote(tg_out.at[mate], tg_in, m_send.at[6], m_recv.at[6], mate_dev)
    tg_copy.start()

    p = iota((32, 512), 1)
    place_of = (lax.div(lax.rem(p, 256), 8) * 2 + core) * 16 + lax.div(p, 256) * 8 + lax.rem(p, 8)
    own512 = jnp.where(iota((32, 512), 0) < 16, place * 16 + iota((32, 512), 0), dp * 16 + iota((32, 512), 0) - 16)
    own_total = jnp.sum(jnp.where(place_of == own512, total, 0.0), axis=1, keepdims=True)
    loss = jnp.log(own_total[16:]) - logit[16:]
    loss_ref[...] = jnp.sum(jnp.where(iota((16, 16), 0) == iota((16, 16), 1), loss, 0.0), axis=0, keepdims=True)

    grad_copy = remote(grad_out, grad_in, m_send.at[7], m_recv.at[7], mate_dev)
    @pl.when(handler)
    def _():
        for h in range(2):
            def rs_wait(s):
                @pl.when(s != place)
                def _():
                    remote(rbuf.at[h, s], rbuf.at[h, s], rs_send.at[h, 0], rs_recv.at[h, s], mate_dev).wait_recv()
            loop(0, 64, rs_wait)
        def add(s, acc):
            return acc + rbuf[:, s].astype(F32)
        u = unpack(lax.fori_loop(0, 64, add, jnp.zeros((2, 48, 128), F32)))
        excess = jnp.exp(logit[:16]) / own_total[:16] - 1.0
        grad = INV_TEMP * ((u + from_tails) / own_total[:16] + excess * pos_emb[:16])
        grad_out[...] = jnp.where(core == 0, grad[8:], grad[:8])
        grad_copy.start()
        qgrad_ref[...] = jnp.where(core == 0, grad[:8], grad[8:])
    @pl.when(jnp.logical_not(handler))
    def _():
        grad_copy.wait_recv()
        qgrad_ref[...] = grad_in[...]
    tg_copy.wait_recv()
    tgrad_ref[...] = jnp.where(core == 0, tg_out[0], tg_out[1]) + tg_in[...]

    @pl.when(handler)
    def _():
        grad_copy.wait_send()
    tg_copy.wait_send()
    keys_copy.wait_send()
    qids_copy.wait_send()
    for h in range(2):
        remote(own_pack.at[h], mate_pack.at[h], m_send.at[h], m_recv.at[h], mate_dev).wait_send()
        remote(gt.at[h, core], gt.at[h, core], m_send.at[4 + h], m_recv.at[4 + h], mate_dev).wait_send()
        loop(1, 64, lambda j: remote(own_pack.at[h], own_pack.at[h], ag_send.at[h, j], m_recv.at[h], mate_dev).wait_send())
        def rs_sent(s):
            @pl.when(lax.div(s, 16) * 32 + lax.rem(2 * s + core, 32) != place)
            def _():
                remote(ubuf.at[h, s], ubuf.at[h, s], rs_send.at[h, s], m_recv.at[h], mate_dev).wait_send()
        loop(0, 32, rs_sent)
    loop(1, 64, lambda j: remote(tot_out, tot_out, tot_send.at[j], m_recv.at[0], mate_dev).wait_send())


MID = 2


def local(token_states, qkv_weight, out_weight, up_weight, down_weight, queue_states, queue_ids, positive, tail_ids):
    vm, anywhere = pl.BlockSpec(memory_space=pltpu.VMEM), pl.BlockSpec(memory_space=pl.ANY)
    dma = pltpu.SemaphoreType.DMA
    loss, qgrad, tgrad = pl.pallas_call(
        step_kernel,
        out_shape=(
            jax.ShapeDtypeStruct((1, 16), F32),
            jax.ShapeDtypeStruct((8, 768), F32),
            jax.ShapeDtypeStruct((16, 768), F32),
        ),
        in_specs=[anywhere] * 5 + [vm] * 4,
        out_specs=(vm, vm, vm),
        scratch_shapes=[
            pltpu.VMEM((768, 2304), BF), pltpu.VMEM((768, 768), BF), pltpu.VMEM((768, 3072), BF), pltpu.VMEM((3072, 768), BF),
            pltpu.VMEM((2, 512, 768), BF),
            pltpu.VMEM((2, 512, 768), BF),
            pltpu.VMEM((2, 1, 512), jnp.int32),
            pltpu.VMEM((8, 512), F32),
            pltpu.VMEM((512, 128), F32),
            pltpu.VMEM((2, 48, 128), BF),
            pltpu.VMEM((2, 48, 128), BF),
            pltpu.VMEM((2, 32, 48, 128), BF),
            pltpu.VMEM((2, 2, 32, 48, 128), BF),
            pltpu.VMEM((512, 768), BF),
            pltpu.VMEM((32, 2, 16, 768), BF),
            pltpu.VMEM((2, 32, 48, 128), BF),
            pltpu.VMEM((2, 64, 48, 128), BF),
            pltpu.VMEM((2, 1, 256), F32),
            pltpu.VMEM((32, 512), F32),
            pltpu.VMEM((1, 512), F32),
            pltpu.VMEM((64, 1, 512), F32),
            pltpu.VMEM((8, 768), F32),
            pltpu.VMEM((8, 768), F32),
            pltpu.VMEM((2, 16, 768), F32),
            pltpu.VMEM((16, 768), F32),
            dma((4,)), dma((2,)), dma((2, 32)), dma((2, 32)), dma((2, 64)), dma((2, 32)), dma((2, 64)),
            dma((64,)), dma((64,)), dma((8,)), dma((8,)),
        ],
        compiler_params=pltpu.CompilerParams(
            collective_id=0, has_side_effects=True, vmem_limit_bytes=60 * 2**20
        ),
    )(token_states.reshape(2, 512, 768), qkv_weight, out_weight, up_weight, down_weight,
      queue_states, queue_ids.reshape(1, 512), positive.reshape(1, 1024), tail_ids.reshape(1, 1024))
    return loss.reshape(16), qgrad, tgrad


def solution(mesh):
    placed = (
        P("tower", "dp", None, None),
        P("tower", None, None, None),
        P("tower", None, None, None),
        P("tower", None, None, None),
        P("tower", None, None, None),
        P(("tower", "dp"), None),
        P(("tower", "dp")),
        P(),
        P(),
    )
    return jax.shard_map(
        local,
        mesh=mesh,
        in_specs=placed,
        out_specs=(P("dp"), P(("tower", "dp"), None), P("dp", None)),
        check_vma=False,
    )
```

time: 922 us -> 83.3 us (0.09)
  the two profiles are of different devices: /device:TPU:4 before, /device:TPU:1 now
where the time goes in v2:
time: 83.3 us; the launch traced here: 83.1 us
  Pallas kernels  78.5 us (94%)
  local copies, waits for them, and re-layouts  3.87 us (5%)
    pallas_call x1, Pallas kernels, local(): pl.pallas_call(step_kernel, out_shape=(jax.ShapeDtypeStruct((1, 16), F32)...  78.5 us
    unnamed x3, local copies, waits for them, and re-layouts  3.87 us

profile of v2, /device:TPU:1, one launch (start us, length us, event | category | flops | bytes accessed | tf_op | source)
XLA Modules:
  0.0 83.1 jit_solution(199312609578110715)
XLA Ops:
  0.6 78.5 %shard_map.112 = (f32[1,16]{1,0:T(1,128)}, f32[8,768]{1,0:T(8,128)}, f32[16,768]{1,0:T(8,128)}) custom-call(bf16[2,512,768]{2,1,0:T(8,128)(2,1)} %bitcast.5, bf16[1,1,768,2304]{3,2,1,0:T(8,128)(2,1)} %qkv_h.1, bf16[1,1,768,768]{3,2,1,0:T(8,128)(2,1)} %out_h.1, bf16[1,1,768,3072]{3,2,1,0:T(8,128)(2,1)} %up_h.1, bf16[1,1,3072,768]{3,2,1,0:T(8,128)(2,1)} %down_h.1, ...), custom_call_target="tpu_custom_call" | custom-call | tf_op jit(solution)/shard_map/pallas_call | solution.py:373
  79.2 1.1 %copy.15 = f32[16]{0:T(128)} copy(f32[16]{0:T(128)} %bitcast.9) | data formatting | bytes 128
  80.3 1.3 %copy.16 = f32[8,768]{1,0:T(8,128)} copy(f32[8,768]{1,0:T(8,128)} %get-tuple-element.13) | data formatting | bytes 49152
  81.6 1.4 %copy.17 = f32[16,768]{1,0:T(8,128)} copy(f32[16,768]{1,0:T(8,128)} %get-tuple-element.14) | data formatting | bytes 98304

commit v3 on v2

--- a/solution.py
+++ b/solution.py
@@ -1,5 +1,5 @@
-import functools
-import jax, jax.numpy as jnp
+import jax
+import jax.numpy as jnp
 from jax import lax
 from jax.experimental import pallas as pl
 from jax.experimental.pallas import tpu as pltpu
@@ -9,20 +9,14 @@
 F32 = jnp.float32
 SEQ = 64
 
+
 def dot(a, b):
     return jnp.dot(a, b, preferred_element_type=F32)
 
+
 def dot_t(a, b):
     return lax.dot_general(a, b, (((1,), (1,)), ((), ())), preferred_element_type=F32)
 
-def gelu(x):
-    a = jnp.abs(x)
-    t = pl.reciprocal(1.0 + (0.3275911 * 0.7071067811865476) * a, approx=True)
-    p = 0.5 * 1.061405429
-    for c in (-1.453152027, 1.421413741, -0.284496736, 0.254829592):
-        p = p * t + 0.5 * c
-    q = p * t * jnp.exp2((x * x) * (-0.5 * 1.4426950408889634))
-    return jnp.maximum(x, 0.0) - a * q
 
 def norm_rows(v):
     avg = jnp.mean(v, axis=-1, keepdims=True)
@@ -30,59 +24,97 @@
     s = jnp.mean(c * c, axis=-1, keepdims=True)
     return c * lax.rsqrt(s + 1e-5)
 
+
 def unit_rows(v):
     return v * lax.rsqrt(jnp.sum(v * v, axis=-1, keepdims=True) + 1e-6)
 
-def enc_chunk(x, wqkv, wout, wup, wdown, waits, mid, fft=768):
-    m = x.shape[0]
-    nt = m // SEQ
-    waits[0]()
+
+def gelu(x):
+    return 0.5 * x * (1.0 + lax.erf(x * 0.7071067811865476))
+
+def att_steps(out, x, wqkv, wout, waits):
+    nt = x.shape[0] // SEQ
     row = lax.broadcasted_iota(jnp.int32, (256, 256), 0) // SEQ
     col = lax.broadcasted_iota(jnp.int32, (256, 256), 1) // SEQ
     ones_bd = jnp.where(row == col, 1.0, 0.0).astype(BF)
-    ctx = []
-    lane = lax.broadcasted_iota(jnp.int32, (SEQ, 128), 1)
-    low = lane < 64
+    low = lax.broadcasted_iota(jnp.int32, (SEQ, 128), 1) < 64
     zero = jnp.zeros((SEQ, 128), BF)
     def bd(t):
         a, b = t[:, :128], t[:, 128:]
         z = jnp.zeros_like(a)
-        rows = [
+        return jnp.concatenate([
             jnp.concatenate([jnp.where(low, a, z), zero], 1),
             jnp.concatenate([jnp.where(low, z, a), zero], 1),
             jnp.concatenate([zero, jnp.where(low, b, z)], 1),
-            jnp.concatenate([zero, jnp.where(low, z, b)], 1),
-        ]
-        return jnp.concatenate(rows, 0)
+            jnp.concatenate([zero, jnp.where(low, z, b)], 1)], 0)
+    ctx = []
+    qkv = []
+    waits[0]()
+    def proj(g):
+        q = dot(x, wqkv[:, g * 256:(g + 1) * 256]).astype(BF) * BF(0.125)
+        k = dot(x, wqkv[:, 768 + g * 256:768 + (g + 1) * 256]).astype(BF)
+        v = dot(x, wqkv[:, 1536 + g * 256:1536 + (g + 1) * 256]).astype(BF)
+        return q, k, v
+    nxt = proj(0)
+    yield
     for g in range(3):
-        q = (dot(x, wqkv[:, g * 256:(g + 1) * 256])).astype(BF) * BF(0.125)
-        k = (dot(x, wqkv[:, 768 + g * 256:768 + (g + 1) * 256])).astype(BF)
-        v = (dot(x, wqkv[:, 1536 + g * 256:1536 + (g + 1) * 256])).astype(BF)
+        q, k, v = nxt
+        if g < 2:
+            nxt = proj(g + 1)
+            yield
         es = []
         for t in range(nt):
             sl = slice(t * SEQ, (t + 1) * SEQ)
             es.append(jnp.exp(dot_t(q[sl], bd(k[sl]))))
+            if t % 2: yield
         e = jnp.concatenate(es, 0)
         p = (e / dot(e.astype(BF), ones_bd)).astype(BF)
+        yield
         cs = []
         for t in range(nt):
             sl = slice(t * SEQ, (t + 1) * SEQ)
             cs.append(dot(p[sl], bd(v[sl])).astype(BF))
+            if t % 2: yield
         ctx.append(jnp.concatenate(cs, 0))
     ctx = jnp.concatenate(ctx, 1)
     waits[1]()
-    normed = norm_rows(x.astype(F32) + dot(ctx, wout[...])).astype(BF)
-    waits[2]()
-    acc = normed.astype(F32)
+    v = x.astype(F32) + dot(ctx, wout[...])
+    yield
+    out["normed"] = norm_rows(v).astype(BF)
+
+def ff_steps(out, normed, wup, wdown, waits, fft=256, nt=256):
+    waits[0]()
+    m = normed.shape[0]
+    acts = []
+    pre = dot(normed, wup[:, 0:fft])
     for j in range(0, 3072, fft):
-        act = gelu(dot(normed, wup[:, j:j + fft])).astype(BF)
-        if j == 0:
-            waits[3]()
-        acc = acc + dot(act, wdown[j:j + fft, :])
-        mid(j // fft)
-    hid = norm_rows(acc).astype(BF).astype(F32)
-    pooled = jnp.mean(hid.reshape(nt, SEQ, 768), axis=1)
-    return unit_rows(pooled)
+        nxt = dot(normed, wup[:, j + fft:j + 2 * fft]) if j + fft < 3072 else None
+        acts.append(gelu(pre).astype(BF))
+        pre = nxt
+        yield
+    act = jnp.concatenate(acts, 1)
+    waits[1]()
+    cols = []
+    for j in range(0, 768, nt):
+        cols.append(normed[:, j:j + nt].astype(F32) + dot(act, wdown[:, j:j + nt]))
+        yield
+    hid = norm_rows(jnp.concatenate(cols, 1)).astype(BF).astype(F32)
+    pooled = jnp.mean(hid.reshape(m // SEQ, SEQ, 768), axis=1)
+    out["emb"] = unit_rows(pooled)
+
+def drain(gen):
+    for _ in gen: pass
+
+def mix(a, na, b, nb):
+    da = db = 0
+    la = lb = True
+    while la or lb:
+        if la and (not lb or da * nb <= db * na):
+            try: next(a); da += 1
+            except StopIteration: la = False
+        elif lb:
+            try: next(b); db += 1
+            except StopIteration: lb = False
 
 MESH = pl.DeviceIdType.MESH
 INV_TEMP = 50.0
@@ -142,9 +174,7 @@
         [(qkv_h, wqkv), (out_h, wout), (up_h, wup), (down_h, wdown)])]
     x_loads = [pltpu.make_async_copy(x_hbm.at[h], xs.at[h], x_sem.at[h]) for h in range(2)]
     x_loads[0].start()
-    for c in loads:
-        c.start()
-    x_loads[1].start()
+    loads[0].start()
 
     def remote(src, dst, ssem, rsem, dev):
         return pltpu.make_async_remote_copy(src_ref=src, dst_ref=dst, send_sem=ssem, recv_sem=rsem, device_id=dev, device_id_type=MESH)
@@ -169,27 +199,37 @@
         ids[1:2, h * 256:(h + 1) * 256] = got[16:17]
         true_col[h * 256:(h + 1) * 256, :] = jnp.transpose(jnp.broadcast_to(got[16:17], (128, 256)))
 
+    def arrived(ref, sem):
+        remote(ref, ref, m_send.at[0], sem, mate_dev).wait_recv()
+
+    def left(ref, sem):
+        remote(ref, ref, sem, m_recv.at[0], mate_dev).wait_send()
+
     def gather_wait(h, side, buf, sems):
-        def one(s):
-            @pl.when(jnp.logical_not((tower == side) & (s == chip)))
-            def _():
-                remote(buf.at[s], buf.at[s], ag_send.at[h, 0], sems.at[h, s], mate_dev).wait_recv()
-        loop(0, 32, one)
-
-    def gather_start(h):
-        def to_all(dst, sems):
-            def one(j):
-                remote(own_pack.at[h], dst, ag_send.at[h, j], sems.at[h, chip], same_core(lax.rem(place + j, 64))).start()
-            loop(1, 64, one)
+        @pl.when(tower == side)
+        def _():
+            arrived(buf.at[pl.ds(0, 31)], sems.at[h])
+        @pl.when(tower != side)
+        def _():
+            arrived(buf, sems.at[h])
+
+    def to_all(h, dst, sems):
+        def one(j):
+            remote(own_pack.at[h], dst, ag_send.at[h], sems.at[h], same_core(lax.rem(place + j, 64))).start()
+        loop(1, 64, one)
+
+    def send_queries(h):
         @pl.when(tower == 0)
         def _():
             gq[h, chip] = own_pack[h]
-            to_all(gq.at[h, chip], agq_recv)
+            to_all(h, gq.at[h, chip], agq_recv)
+        remote(own_pack.at[h], mate_pack.at[h], m_send.at[h], m_recv.at[h], mate_dev).start()
+
+    def send_tails(h):
         @pl.when(tower == 1)
         def _():
             gt[h, core, chip] = own_pack[h]
-            to_all(gt.at[h, core, chip], agt_recv)
-        remote(own_pack.at[h], mate_pack.at[h], m_send.at[h], m_recv.at[h], mate_dev).start()
+            to_all(h, gt.at[h, core, chip], agt_recv)
 
     def queue_part(h):
         gather_wait(h, 0, gq.at[h], agq_recv)
@@ -214,43 +254,53 @@
                 rbuf[h, place] = ubuf[h, s]
             @pl.when(dest != place)
             def _():
-                remote(ubuf.at[h, s], rbuf.at[h, place], rs_send.at[h, s], rs_recv.at[h, place], same_core(dest)).start()
+                remote(ubuf.at[h, s], rbuf.at[h, place], rs_send.at[h], rs_recv.at[h], same_core(dest)).start()
         loop(0, 32, one)
 
     keys_copy = remote(keys.at[0], keys.at[1], m_send.at[2], m_recv.at[2], mate_dev)
     qids_copy = remote(qids.at[0], qids.at[1], m_send.at[3], m_recv.at[3], mate_dev)
 
+    def nothing():
+        pass
+
     def half(h):
-        def waiter(c):
-            def f():
-                @pl.when(h == 0)
-                def _():
-                    c.wait()
-                    if c is loads[1]:
-                        pl.semaphore_wait(barrier, 64)
-            return f
-        def mid(j):
-            if j == MID:
-                @pl.when(h == 1)
-                def _():
-                    keys_copy.wait_recv()
-                    qids_copy.wait_recv()
-                    queue_part(0)
-        pltpu.make_async_copy(x_hbm.at[h], xs.at[h], x_sem.at[h]).wait()
-        emb = enc_chunk(xs[h], wqkv, wout, wup, wdown, [waiter(c) for c in loads], mid)
-        own_pack[h] = pack(emb).astype(BF)
-        @pl.when(h == 0)
-        def _():
+        out = {}
+        x_loads[h].wait()
+        for _ in att_steps(out, xs[h], wqkv, wout, (loads[0].wait, loads[1].wait) if h == 0 else (nothing, nothing)):
+            pass
+        if h == 0:
+            pl.semaphore_wait(barrier, 64)
             keys_copy.start()
             qids_copy.start()
-        gather_start(h)
-    loop(0, 2, half)
+        elif not EARLY:
+            send_tails(0)
+        for i, _ in enumerate(ff_steps(out, out["normed"], wup, wdown, (loads[2].wait, loads[3].wait) if h == 0 else (nothing, nothing))):
+            if h == 1 and i == MID:
+                keys_copy.wait_recv()
+                qids_copy.wait_recv()
+                queue_part(0)
+        own_pack[h] = pack(out["emb"]).astype(BF)
+        send_queries(h)
+        if h == 0 and EARLY or h == 1 and not LATE:
+            send_tails(h)
+
+    for c in loads[1:]:
+        c.start()
+    x_loads[1].start()
+    half(0)
+    half(1)
+    if MID is None:
+        keys_copy.wait_recv()
+        qids_copy.wait_recv()
+        queue_part(0)
 
     def pack_wait(h):
         remote(mate_pack.at[h], mate_pack.at[h], m_send.at[h], m_recv.at[h], mate_dev).wait_recv()
     pack_wait(0)
     pack_wait(1)
     queue_part(1)
+    if LATE == 1:
+        send_tails(1)
 
     pos_q, true_q = ids[0:1, :].astype(jnp.int32), ids[1:2, :]
     row = iota((32, 512), 0)
@@ -272,7 +322,10 @@
     tail_part = jnp.sum(tail_exp[...], axis=0, keepdims=True)
     tot_out[...] = total + jnp.where(tower == 1, tail_part, 0.0)
     tot_in[place] = tot_out[...]
-    loop(1, 64, lambda j: remote(tot_out, tot_in.at[place], tot_send.at[j], tot_recv.at[place], same_core(lax.rem(place + j, 64))).start())
+    loop(1, 64, lambda j: remote(tot_out, tot_in.at[place], tot_send.at[0], tot_recv.at[0], same_core(lax.rem(place + j, 64))).start())
+
+    if LATE == 2:
+        send_tails(1)
 
     for h in range(2):
         gather_wait(h, 1, gt.at[h, core], agt_recv)
@@ -303,11 +356,21 @@
     own_e = jnp.where(at_pos[:16] | (tid == own_true[:16]), 0.0, jnp.exp(own_s))
     from_tails = dot(own_e.astype(BF), all_tails)
 
-    def tot_wait(s):
-        @pl.when(s != place)
-        def _():
-            remote(tot_in.at[s], tot_in.at[s], tot_send.at[0], tot_recv.at[s], mate_dev).wait_recv()
-    loop(0, 64, tot_wait)
+    for h in range(2):
+        left(rbuf.at[h, pl.ds(0, 63)], ag_send.at[h])
+        @pl.when(handler)
+        def _():
+            left(ubuf.at[h, pl.ds(0, 31)], rs_send.at[h])
+        @pl.when(jnp.logical_not(handler))
+        def _():
+            left(ubuf.at[h], rs_send.at[h])
+        left(mate_pack.at[h], m_send.at[h])
+        left(gt.at[h, core], m_send.at[4 + h])
+    keys_copy.wait_send()
+    qids_copy.wait_send()
+    left(tot_in.at[pl.ds(0, 63)], tot_send.at[0])
+
+    arrived(tot_in.at[pl.ds(0, 63)], tot_recv.at[0])
     total = jnp.sum(tot_in[...], axis=0)
 
     weights = (tail_exp[...] / total - is_pos.astype(F32)).astype(BF)
@@ -326,11 +389,7 @@
     @pl.when(handler)
     def _():
         for h in range(2):
-            def rs_wait(s):
-                @pl.when(s != place)
-                def _():
-                    remote(rbuf.at[h, s], rbuf.at[h, s], rs_send.at[h, 0], rs_recv.at[h, s], mate_dev).wait_recv()
-            loop(0, 64, rs_wait)
+            arrived(rbuf.at[h, pl.ds(0, 63)], rs_recv.at[h])
         def add(s, acc):
             return acc + rbuf[:, s].astype(F32)
         u = unpack(lax.fori_loop(0, 64, add, jnp.zeros((2, 48, 128), F32)))
@@ -350,21 +409,12 @@
     def _():
         grad_copy.wait_send()
     tg_copy.wait_send()
-    keys_copy.wait_send()
-    qids_copy.wait_send()
-    for h in range(2):
-        remote(own_pack.at[h], mate_pack.at[h], m_send.at[h], m_recv.at[h], mate_dev).wait_send()
-        remote(gt.at[h, core], gt.at[h, core], m_send.at[4 + h], m_recv.at[4 + h], mate_dev).wait_send()
-        loop(1, 64, lambda j: remote(own_pack.at[h], own_pack.at[h], ag_send.at[h, j], m_recv.at[h], mate_dev).wait_send())
-        def rs_sent(s):
-            @pl.when(lax.div(s, 16) * 32 + lax.rem(2 * s + core, 32) != place)
-            def _():
-                remote(ubuf.at[h, s], ubuf.at[h, s], rs_send.at[h, s], m_recv.at[h], mate_dev).wait_send()
-        loop(0, 32, rs_sent)
-    loop(1, 64, lambda j: remote(tot_out, tot_out, tot_send.at[j], m_recv.at[0], mate_dev).wait_send())
-
-
-MID = 2
+
+
+MID = 11
+LATE = 0
+VM = 60
+EARLY = False
 
 
 def local(token_states, qkv_weight, out_weight, up_weight, down_weight, queue_states, queue_ids, positive, tail_ids):
@@ -402,11 +452,11 @@
             pltpu.VMEM((8, 768), F32),
             pltpu.VMEM((2, 16, 768), F32),
             pltpu.VMEM((16, 768), F32),
-            dma((4,)), dma((2,)), dma((2, 32)), dma((2, 32)), dma((2, 64)), dma((2, 32)), dma((2, 64)),
-            dma((64,)), dma((64,)), dma((8,)), dma((8,)),
+            dma((4,)), dma((2,)), dma((2,)), dma((2,)), dma((2,)), dma((2,)), dma((2,)),
+            dma((1,)), dma((1,)), dma((8,)), dma((8,)),
         ],
         compiler_params=pltpu.CompilerParams(
-            collective_id=0, has_side_effects=True, vmem_limit_bytes=60 * 2**20
+            collective_id=0, has_side_effects=True, vmem_limit_bytes=VM * 2**20
         ),
     )(token_states.reshape(2, 512, 768), qkv_weight, out_weight, up_weight, down_weight,
       queue_states, queue_ids.reshape(1, 512), positive.reshape(1, 1024), tail_ids.reshape(1, 1024))

time: 83.3 us -> 72 us (0.86)
  Pallas kernels: 78.5 us -> 67.3 us
    pallas_call x1, Pallas kernels: 78.5 us -> 67.3 us  [local(): pl.pallas_call(step_kernel, out_shape=(jax.ShapeDtypeStruct((1, 16), F32)...]
where the time goes in v3:
time: 72 us; the launch traced here: 71.8 us
  Pallas kernels  67.3 us (93%)
  local copies, waits for them, and re-layouts  3.87 us (5%)
    pallas_call x1, Pallas kernels, local(): pl.pallas_call(step_kernel, out_shape=(jax.ShapeDtypeStruct((1, 16), F32)...  67.3 us
    unnamed x3, local copies, waits for them, and re-layouts  3.87 us

profile of v3, /device:TPU:1, one launch (start us, length us, event | category | flops | bytes accessed | tf_op | source)
XLA Modules:
  0.0 71.8 jit_solution(3486759189268699547)
XLA Ops:
  0.6 67.3 %shard_map.112 = (f32[1,16]{1,0:T(1,128)}, f32[8,768]{1,0:T(8,128)}, f32[16,768]{1,0:T(8,128)}) custom-call(bf16[2,512,768]{2,1,0:T(8,128)(2,1)} %bitcast.5, bf16[1,1,768,2304]{3,2,1,0:T(8,128)(2,1)} %qkv_h.1, bf16[1,1,768,768]{3,2,1,0:T(8,128)(2,1)} %out_h.1, bf16[1,1,768,3072]{3,2,1,0:T(8,128)(2,1)} %up_h.1, bf16[1,1,3072,768]{3,2,1,0:T(8,128)(2,1)} %down_h.1, ...), custom_call_target="tpu_custom_call" | custom-call | tf_op jit(solution)/shard_map/pallas_call | solution.py:423
  67.9 1.1 %copy.15 = f32[16]{0:T(128)} copy(f32[16]{0:T(128)} %bitcast.9) | data formatting | bytes 128
  69.0 1.3 %copy.16 = f32[8,768]{1,0:T(8,128)} copy(f32[8,768]{1,0:T(8,128)} %get-tuple-element.13) | data formatting | bytes 49152
  70.3 1.4 %copy.17 = f32[16,768]{1,0:T(8,128)} copy(f32[16,768]{1,0:T(8,128)} %get-tuple-element.14) | data formatting | bytes 98304

commit v4 on v3

--- a/solution.py
+++ b/solution.py
@@ -215,7 +215,7 @@
 
     def to_all(h, dst, sems):
         def one(j):
-            remote(own_pack.at[h], dst, ag_send.at[h], sems.at[h], same_core(lax.rem(place + j, 64))).start()
+            remote(own_pack.at[h], dst, ag_send.at[h], sems.at[h], same_core(lax.rem(place + HOP * j, 64))).start()
         loop(1, 64, one)
 
     def send_queries(h):
@@ -247,7 +247,8 @@
         qtot[h] = to_row(total)
         for s in range(32):
             ubuf[h, s] = pack(u[s * 8:(s + 1) * 8]).astype(BF)
-        def one(s):
+        def one(j):
+            s = lax.rem(j * STRIDE + chip, 32)
             dest = lax.div(s, 16) * 32 + lax.rem(2 * s + core, 32)
             @pl.when(dest == place)
             def _():
@@ -322,7 +323,7 @@
     tail_part = jnp.sum(tail_exp[...], axis=0, keepdims=True)
     tot_out[...] = total + jnp.where(tower == 1, tail_part, 0.0)
     tot_in[place] = tot_out[...]
-    loop(1, 64, lambda j: remote(tot_out, tot_in.at[place], tot_send.at[0], tot_recv.at[0], same_core(lax.rem(place + j, 64))).start())
+    loop(1, 64, lambda j: remote(tot_out, tot_in.at[place], tot_send.at[0], tot_recv.at[0], same_core(lax.rem(place + HOP * j, 64))).start())
 
     if LATE == 2:
         send_tails(1)
@@ -388,11 +389,14 @@
     grad_copy = remote(grad_out, grad_in, m_send.at[7], m_recv.at[7], mate_dev)
     @pl.when(handler)
     def _():
-        for h in range(2):
+        def summed(h):
             arrived(rbuf.at[h, pl.ds(0, 63)], rs_recv.at[h])
-        def add(s, acc):
-            return acc + rbuf[:, s].astype(F32)
-        u = unpack(lax.fori_loop(0, 64, add, jnp.zeros((2, 48, 128), F32)))
+            def add(s, acc):
+                for i in range(4):
+                    acc = acc + rbuf[h, s * 4 + i].astype(F32)
+                return acc
+            return lax.fori_loop(0, 16, add, jnp.zeros((48, 128), F32))
+        u = unpack(jnp.stack([summed(0), summed(1)]))
         excess = jnp.exp(logit[:16]) / own_total[:16] - 1.0
         grad = INV_TEMP * ((u + from_tails) / own_total[:16] + excess * pos_emb[:16])
         grad_out[...] = jnp.where(core == 0, grad[8:], grad[:8])
@@ -412,6 +416,8 @@
 
 
 MID = 11
+STRIDE = 5
+HOP = 21
 LATE = 0
 VM = 60
 EARLY = False
@@ -460,6 +466,15 @@
         ),
     )(token_states.reshape(2, 512, 768), qkv_weight, out_weight, up_weight, down_weight,
       queue_states, queue_ids.reshape(1, 512), positive.reshape(1, 1024), tail_ids.reshape(1, 1024))
+    def finish(*refs):
+        for src, dst in zip(refs[:3], refs[3:]):
+            dst[...] = src[...]
+    loss, qgrad, tgrad = pl.pallas_call(
+        finish,
+        out_shape=tuple(jax.ShapeDtypeStruct(v.shape, F32) for v in (loss, qgrad, tgrad)),
+        in_specs=[vm] * 3,
+        out_specs=(vm, vm, vm),
+    )(loss, qgrad, tgrad)
     return loss.reshape(16), qgrad, tgrad
 
 

time: 72 us -> 68.8 us (0.956)
  local copies, waits for them, and re-layouts: 3.87 us -> 0 us
    unnamed x3 -> x0, local copies, waits for them, and re-layouts: 3.87 us -> none
    pallas_call x0 -> x1, Pallas kernels: none -> 1.46 us  [local(): pl.pallas_call(finish, out_shape=tuple((jax.ShapeDtypeStruct(v.shape, F32...]
    pallas_call x1, Pallas kernels: 67.3 us -> 66.5 us  [local(): pl.pallas_call(step_kernel, out_shape=(jax.ShapeDtypeStruct((1, 16), F32)...]
where the time goes in v4:
time: 68.8 us; the launch traced here: 68.6 us
  Pallas kernels  67.9 us (99%)
    pallas_call x1, Pallas kernels, local(): pl.pallas_call(step_kernel, out_shape=(jax.ShapeDtypeStruct((1, 16), F32)...  66.5 us
    pallas_call x1, Pallas kernels, local(): pl.pallas_call(finish, out_shape=tuple((jax.ShapeDtypeStruct(v.shape, F32...  1.46 us

profile of v4, /device:TPU:1, one launch (start us, length us, event | category | flops | bytes accessed | tf_op | source)
XLA Modules:
  0.0 68.6 jit_solution(1523922812972180234)
XLA Ops:
  0.6 66.5 %shard_map.112 = (f32[1,16]{1,0:T(1,128)}, f32[8,768]{1,0:T(8,128)}, f32[16,768]{1,0:T(8,128)}) custom-call(bf16[2,512,768]{2,1,0:T(8,128)(2,1)} %bitcast.5, bf16[1,1,768,2304]{3,2,1,0:T(8,128)(2,1)} %qkv_h.1, bf16[1,1,768,768]{3,2,1,0:T(8,128)(2,1)} %out_h.1, bf16[1,1,768,3072]{3,2,1,0:T(8,128)(2,1)} %up_h.1, bf16[1,1,3072,768]{3,2,1,0:T(8,128)(2,1)} %down_h.1, ...), custom_call_target="tpu_custom_call" | custom-call | tf_op jit(solution)/shard_map/pallas_call | solution.py:429
  67.1 1.5 %shard_map.113 = (f32[1,16]{1,0:T(1,128)}, f32[8,768]{1,0:T(8,128)}, f32[16,768]{1,0:T(8,128)}) custom-call(f32[1,16]{1,0:T(1,128)} %get-tuple-element.9.refs_0_, f32[8,768]{1,0:T(8,128)} %get-tuple-element.10.refs_1_, f32[16,768]{1,0:T(8,128)} %get-tuple-element.11.refs_2_), custom_call_target="tpu_custom_call" | custom-call | tf_op jit(solution)/shard_map/pallas_call | solution.py:472

commit v5 on v4

--- a/solution.py
+++ b/solution.py
@@ -82,23 +82,20 @@
     yield
     out["normed"] = norm_rows(v).astype(BF)
 
-def ff_steps(out, normed, wup, wdown, waits, fft=256, nt=256):
+def ff_steps(out, normed, wup, wdown, waits, fft=768):
     waits[0]()
     m = normed.shape[0]
-    acts = []
+    acc = normed.astype(F32)
     pre = dot(normed, wup[:, 0:fft])
     for j in range(0, 3072, fft):
         nxt = dot(normed, wup[:, j + fft:j + 2 * fft]) if j + fft < 3072 else None
-        acts.append(gelu(pre).astype(BF))
+        act = gelu(pre).astype(BF)
         pre = nxt
+        if j == 0:
+            waits[1]()
+        acc = acc + dot(act, wdown[j:j + fft, :])
         yield
-    act = jnp.concatenate(acts, 1)
-    waits[1]()
-    cols = []
-    for j in range(0, 768, nt):
-        cols.append(normed[:, j:j + nt].astype(F32) + dot(act, wdown[:, j:j + nt]))
-        yield
-    hid = norm_rows(jnp.concatenate(cols, 1)).astype(BF).astype(F32)
+    hid = norm_rows(acc).astype(BF).astype(F32)
     pooled = jnp.mean(hid.reshape(m // SEQ, SEQ, 768), axis=1)
     out["emb"] = unit_rows(pooled)
 
@@ -295,10 +292,25 @@
         qids_copy.wait_recv()
         queue_part(0)
 
+    def forward_tails(h):
+        gather_wait(h, 1, gt.at[h, core], agt_recv)
+        remote(gt.at[h, core], gt.at[h, core], m_send.at[4 + h], m_recv.at[4 + h], mate_dev).start()
+
     def pack_wait(h):
         remote(mate_pack.at[h], mate_pack.at[h], m_send.at[h], m_recv.at[h], mate_dev).wait_recv()
     pack_wait(0)
     pack_wait(1)
+    forward_tails(0)
+
+    rows = iota((32, 1024), 0)
+    lane = iota((32, 1024), 1)
+    own = jnp.where(rows < 16, place * 16 + rows, dp * 16 + rows - 16)
+    sel = lane == own
+    own_pos = jnp.sum(jnp.where(sel, pos.astype(F32), 0.0), axis=1, keepdims=True).astype(jnp.int32)
+    own_true = jnp.sum(jnp.where(sel, true_row, 0.0), axis=1, keepdims=True)
+    at_pos = hot(lane == own_pos)
+    skip = (lane == own_pos) | (tid == own_true)
+
     queue_part(1)
     if LATE == 1:
         send_tails(1)
@@ -328,9 +340,7 @@
     if LATE == 2:
         send_tails(1)
 
-    for h in range(2):
-        gather_wait(h, 1, gt.at[h, core], agt_recv)
-        remote(gt.at[h, core], gt.at[h, core], m_send.at[4 + h], m_recv.at[4 + h], mate_dev).start()
+    forward_tails(1)
     for h in range(2):
         remote(gt.at[h, mate], gt.at[h, mate], m_send.at[4 + h], m_recv.at[4 + h], mate_dev).wait_recv()
     @pl.when(tower == 0)
@@ -341,21 +351,14 @@
         tails[:, who] = jnp.concatenate(halves, axis=1).astype(BF)
     all_tails = tails[...].reshape(1024, 768)
 
-    rows = iota((32, 1024), 0)
-    lane = iota((32, 1024), 1)
-    own = jnp.where(rows < 16, place * 16 + rows, dp * 16 + rows - 16)
-    sel = lane == own
-    own_pos = jnp.sum(jnp.where(sel, pos.astype(F32), 0.0), axis=1, keepdims=True).astype(jnp.int32)
-    own_true = jnp.sum(jnp.where(sel, true_row, 0.0), axis=1, keepdims=True)
     def query_rows(d):
         return jnp.concatenate([unpack(gq[h, pl.ds(lax.div(d, 2), 1)].astype(F32)) for h in range(2)], axis=0)
     own_q = jnp.concatenate([query_rows(place), query_rows(dp)], axis=0)
-    at_pos = lane == own_pos
-    pos_emb = dot(hot(at_pos), all_tails)
+    own_s = INV_TEMP * dot_t(own_q[:16].astype(BF), all_tails)
+    own_e = jnp.where(skip[:16], 0.0, jnp.exp(own_s))
+    taken = dot(jnp.concatenate([own_e.astype(BF), at_pos], axis=0), all_tails)
+    from_tails, pos_emb = taken[:16], taken[16:]
     logit = INV_TEMP * jnp.sum(own_q * pos_emb, axis=1, keepdims=True) - 1.0
-    own_s = INV_TEMP * dot_t(own_q[:16].astype(BF), all_tails)
-    own_e = jnp.where(at_pos[:16] | (tid == own_true[:16]), 0.0, jnp.exp(own_s))
-    from_tails = dot(own_e.astype(BF), all_tails)
 
     for h in range(2):
         left(rbuf.at[h, pl.ds(0, 63)], ag_send.at[h])
@@ -415,7 +418,7 @@
     tg_copy.wait_send()
 
 
-MID = 11
+MID = 2
 STRIDE = 5
 HOP = 21
 LATE = 0

time: 68.8 us -> 67.1 us (0.975)
  Pallas kernels: 67.9 us -> 66.3 us
    pallas_call x1, Pallas kernels: 66.5 us -> 64.8 us  [local(): pl.pallas_call(step_kernel, out_shape=(jax.ShapeDtypeStruct((1, 16), F32)...]
where the time goes in v5:
time: 67.1 us; the launch traced here: 66.9 us
  Pallas kernels  66.3 us (99%)
    pallas_call x1, Pallas kernels, local(): pl.pallas_call(step_kernel, out_shape=(jax.ShapeDtypeStruct((1, 16), F32)...  64.8 us
    pallas_call x1, Pallas kernels, local(): pl.pallas_call(finish, out_shape=tuple((jax.ShapeDtypeStruct(v.shape, F32...  1.46 us

profile of v5, /device:TPU:1, one launch (start us, length us, event | category | flops | bytes accessed | tf_op | source)
XLA Modules:
  0.0 66.9 jit_solution(5313863127126599817)
XLA Ops:
  0.6 64.8 %shard_map.112 = (f32[1,16]{1,0:T(1,128)}, f32[8,768]{1,0:T(8,128)}, f32[16,768]{1,0:T(8,128)}) custom-call(bf16[2,512,768]{2,1,0:T(8,128)(2,1)} %bitcast.5, bf16[1,1,768,2304]{3,2,1,0:T(8,128)(2,1)} %qkv_h.1, bf16[1,1,768,768]{3,2,1,0:T(8,128)(2,1)} %out_h.1, bf16[1,1,768,3072]{3,2,1,0:T(8,128)(2,1)} %up_h.1, bf16[1,1,3072,768]{3,2,1,0:T(8,128)(2,1)} %down_h.1, ...), custom_call_target="tpu_custom_call" | custom-call | tf_op jit(solution)/shard_map/pallas_call | solution.py:432
  65.4 1.5 %shard_map.113 = (f32[1,16]{1,0:T(1,128)}, f32[8,768]{1,0:T(8,128)}, f32[16,768]{1,0:T(8,128)}) custom-call(f32[1,16]{1,0:T(1,128)} %get-tuple-element.9.refs_0_, f32[8,768]{1,0:T(8,128)} %get-tuple-element.10.refs_1_, f32[16,768]{1,0:T(8,128)} %get-tuple-element.11.refs_2_), custom_call_target="tpu_custom_call" | custom-call | tf_op jit(solution)/shard_map/pallas_call | solution.py:475
